TPU v7x, 512 devices: a whole 4x4x16 slice. The times are simulated.
512 devices in a mesh: seg: 16 (over z_hi, x), coil: 32 (over y, z_lo, core).
Axes of the slice: x: 4, y: 4, z: 16 (z_hi: 4, z_lo: 4; z = z_hi * 4 + z_lo), core: 2. Of those that a mesh axis runs over, the one named last changes fastest.
Arguments:
- image_estimate: bfloat16 [1, 384, 768], replicated, may hold values from -6 to 6
- coil_maps: bfloat16 [32, 384, 768], P('coil'), may hold values from -3 to 3
- field_map: float32 [384, 384], replicated, may hold values from -3 to 3
- interp_rows: bfloat16 [1, 256, 384], replicated, may hold values from -0.3125 to 0.3125
- interp_cols: bfloat16 [1, 128, 384], replicated, may hold values from -0.3125 to 0.3125
- measured: bfloat16 [32, 1, 256, 256], P('coil'), may hold values from -6 to 6
- sample_time: int32 [1, 256], replicated, may hold values from 0 to 60
- sample_count: int32 [1], replicated, may hold values from 128 to 256
Outputs:
- gradient: float32 [1, 384, 768], P(None, 'coil', 'seg')
- residual: float32 [32, 1, 256, 256], P('coil', None, 'seg')
Inputs may be any that keep to these rules, and one draw needn't show every extreme that they name: sample_time counts the sample clock, 4 steps to a segment. Rows below sample_count[p] of partition p are acquired.
All inputs are finite; a program needn't handle non-finite values.
Results may differ from a plain program's by a relative error of at most 0.017.
Values sent between devices are 32-bit elements; how exact they have to be, the bound alone decides.
A program may use at most 64 MiB of HBM per device.

v0:
```python
import math

import jax
import jax.numpy as jnp
from jax import lax
from jax.sharding import PartitionSpec as P

SUBSTEPS = 4


def dft_tables(length):
    indices = jnp.arange(length, dtype=jnp.int32)
    wrapped = indices[:, None] * indices[None, :] % length
    angles = wrapped.astype(jnp.float32) * (2.0 * math.pi / length)
    factor = 1.0 / math.sqrt(length)
    return (jnp.cos(angles) * factor, jnp.sin(angles) * factor)


def shards(
    image_estimate,
    coil_maps,
    field_map,
    interp_rows,
    interp_cols,
    measured,
    sample_time,
    sample_count,
):
    segment = lax.axis_index("seg")
    seg_total = lax.axis_size("seg")
    coil_total = lax.axis_size("coil")
    pixels = field_map.shape[0]
    row_total = interp_rows.shape[1]
    col_total = interp_cols.shape[1]
    own_rows = row_total // seg_total
    start_row = segment * own_rows
    cosine, sine = dft_tables(pixels)
    stacked_table = jnp.concatenate([cosine, sine], axis=0).astype(jnp.bfloat16)
    forward_right = jnp.concatenate(
        [jnp.concatenate([cosine, -sine], 1), jnp.concatenate([sine, cosine], 1)], 0
    ).astype(jnp.bfloat16)
    inverse_right = jnp.concatenate(
        [jnp.concatenate([cosine, sine], 1), jnp.concatenate([-sine, cosine], 1)], 0
    ).astype(jnp.bfloat16)
    offset = segment.astype(jnp.float32) - 0.5 * (seg_total - 1)
    angles = field_map * offset
    phase_re = jnp.cos(angles)
    phase_im = jnp.sin(angles)
    maps = coil_maps[0].astype(jnp.float32)
    sens_re = maps[:, :pixels]
    sens_im = maps[:, pixels:]
    comb_re = sens_re * phase_re - sens_im * phase_im
    comb_im = sens_re * phase_im + sens_im * phase_re
    factor = coil_total ** (-0.5)
    row_ids = jnp.arange(row_total, dtype=jnp.int32)
    current = image_estimate[0].astype(jnp.float32)
    cur_re = current[:, :pixels]
    cur_im = current[:, pixels:]
    weighted = jnp.concatenate(
        [cur_re * comb_re - cur_im * comb_im, cur_re * comb_im + cur_im * comb_re], 1
    ).astype(jnp.bfloat16)
    products = jnp.dot(stacked_table, weighted, preferred_element_type=jnp.float32)
    cos_part = products[:pixels]
    sin_part = products[pixels:]
    rows_ft = jnp.concatenate(
        [cos_part[:, :pixels] + sin_part[:, pixels:], cos_part[:, pixels:] - sin_part[:, :pixels]],
        1,
    ).astype(jnp.bfloat16)
    kspace = jnp.dot(rows_ft, forward_right, preferred_element_type=jnp.float32).astype(
        jnp.bfloat16
    )
    picked = jnp.dot(interp_rows[0], kspace, preferred_element_type=jnp.float32).astype(
        jnp.bfloat16
    )
    sampled = jnp.einsum(
        "mrn,kn->mrk",
        picked.reshape(row_total, 2, pixels),
        interp_cols[0],
        preferred_element_type=jnp.float32,
    ).reshape(row_total, 2 * col_total)
    sample_steps = sample_time[0].astype(jnp.float32)
    weights = jnp.maximum(
        0.0, 1.0 - jnp.abs(sample_steps - (segment * SUBSTEPS).astype(jnp.float32)) / SUBSTEPS
    )
    partial_sum = weights[:, None] * sampled
    sampled_mask = (row_ids < sample_count[0]).astype(jnp.float32)[:, None]
    data_rows = measured[0, 0].astype(jnp.float32)
    totals = lax.psum(partial_sum, "seg")
    misfit = sampled_mask * (totals - data_rows)
    misfit_own = lax.dynamic_slice_in_dim(misfit, start_row, own_rows, 0)
    back_weighted = (weights[:, None] * misfit).astype(jnp.bfloat16)
    spread = lax.dot_general(
        interp_rows[0], back_weighted, (((0,), (0,)), ((), ())), preferred_element_type=jnp.float32
    ).astype(jnp.bfloat16)
    gridded = (
        jnp.einsum(
            "nrk,kj->nrj",
            spread.reshape(pixels, 2, col_total),
            interp_cols[0],
            preferred_element_type=jnp.float32,
        )
        .reshape(pixels, 2 * pixels)
        .astype(jnp.bfloat16)
    )
    back_products = jnp.dot(stacked_table, gridded, preferred_element_type=jnp.float32)
    cos_back = back_products[:pixels]
    sin_back = back_products[pixels:]
    back_rows = jnp.concatenate(
        [cos_back[:, :pixels] - sin_back[:, pixels:], cos_back[:, pixels:] + sin_back[:, :pixels]],
        1,
    ).astype(jnp.bfloat16)
    back_image = jnp.dot(back_rows, inverse_right, preferred_element_type=jnp.float32)
    image_re = back_image[:, :pixels]
    image_im = back_image[:, pixels:]
    image_term = factor * jnp.concatenate(
        [comb_re * image_re + comb_im * image_im, comb_re * image_im - comb_im * image_re], 1
    )
    across = lax.psum_scatter(image_term, "coil", scatter_dimension=0, tiled=True)
    reduced = lax.psum_scatter(across, "seg", scatter_dimension=1, tiled=True)
    gradients = [reduced]
    residuals = [misfit_own]
    gradient = jnp.stack(gradients, axis=0)
    residual = jnp.stack(residuals, axis=0)[None]
    return (gradient, residual)


def solution(mesh):
    in_specs = (P(), P("coil", None, None), P(), P(), P(), P("coil", None, None, None), P(), P())
    out_specs = (P(None, "coil", "seg"), P("coil", None, "seg", None))
    return jax.shard_map(shards, mesh=mesh, in_specs=in_specs, out_specs=out_specs, check_vma=False)
```

profile of v0, /device:TPU:1, one launch (start us, length us, event | category | flops | bytes accessed | tf_op | source)
XLA Modules:
  0.0 455.2 jit_solution(10161998638075263033)
XLA Ops:
  7.2 3.0 negate_convert_fusion
  10.2 2.6 multiply_convert_fusion
  12.8 1.3 bitcast_convert_fusion
  14.1 2.4 subtract_convert_fusion
  16.7 0.8 fusion.21
  17.6 2.3 fusion.2
  20.6 0.8 broadcast_multiply_fusion
  22.2 195.8 %all-reduce.4.cloned.1.call-done = f32[256,256]{1,0:T(8,128)} async-done(((f32[256,256]{1,0:T(8,128)}), f32[256,256]{1,0:T(8,128)}) %all-reduce.4.cloned.1.call-update) | async-done | bytes 262160 | tf_op jit(solution)/shard_map/psum | solution.py:88
  217.9 1.0 fusion.39
  220.6 0.8 copy-done.4
  222.4 86.3 %fusion = f32[16,768]{1,0:T(8,128)S(1)} fusion(f32[384,768]{1,0:T(8,128)S(1)} %maximum_multiply_fusion), kind=kCustom, calls=%all-reduce-scatter | all-reduce-scatter fusion | flops 393217 | bytes 1230848
  308.8 1.3 collective-permute-start.6
  310.1 1.3 collective-permute-start.5
  311.4 1.3 collective-permute-start.7
  312.7 1.3 collective-permute-start.4
  314.0 12.0 %collective-permute-start.3 = (f32[16,768]{1,0:T(8,128)S(1)}, f32[16,768]{1,0:T(8,128)S(1)}, u32[]{:S(2)}, u32[]{:S(2)}) collective-permute-start(f32[16,768]{1,0:T(8,128)S(1)} %fusion), channel_id=1, source_target_pairs={{0,4},{1,5},{2,6},{3,7},{4,8},{5,9},{6,10},{7,11},{8,12},{9,13},{1... | collective-permute-start | bytes 147464
  326.0 1.3 collective-permute-start.2
  327.3 4.0 collective-permute-start.1
  331.3 2.2 collective-permute-start
  333.5 1.3 dynamic-slice.4
  335.5 1.0 concatenate.54
  336.6 0.9 copy.24
  338.2 108.7 %reduce-scatter.6.cloned.1.call-done = f32[48,12]{1,0:T(8,128)} async-done(((f32[768,12]{1,0:T(8,128)}), f32[48,12]{1,0:T(8,128)}) %reduce-scatter.6.cloned.1.call-update) | async-done | bytes 2320
  446.9 0.8 copy.25
  (42 shorter events, 4.9 us)
Async XLA Ops:
  7.2 10.5 %copy-start = (bf16[1,256,384]{2,1,0:T(8,128)(2,1)S(1)}, bf16[1,256,384]{2,1,0:T(8,128)(2,1)}, u32[]{:S(2)}) copy-start(bf16[1,256,384]{2,1,0:T(8,128)(2,1)} %param.11) | copy-start | bytes 589828
  7.2 5.6 %copy-start.2 = (bf16[1,384,768]{2,1,0:T(8,128)(2,1)S(1)}, bf16[1,384,768]{2,1,0:T(8,128)(2,1)}, u32[]{:S(2)}) copy-start(bf16[1,384,768]{2,1,0:T(8,128)(2,1)} %param.8) | copy-start | bytes 1769476
  7.2 210.7 %all-reduce.4.cloned.1.call-start = ((), (), s32[]{:S(2)}) async-start(), calls=%async_computation.1 | async-start | bytes 524288 | tf_op jit(solution)/shard_map/psum | solution.py:88
  12.8 1.3 copy-start.1
  17.6 2.3 copy-start.3
  19.9 0.7 copy-start.6
  19.9 198.0 %copy-start.5 = (bf16[1,1,256,256]{3,2,1,0:T(8,128)(2,1)S(1)}, bf16[1,1,256,256]{3,2,1,0:T(8,128)(2,1)}, u32[]{:S(2)}) copy-start(bf16[1,1,256,256]{3,2,1,0:T(8,128)(2,1)} %param.13) | copy-start | bytes 393220
  21.4 425.5 %reduce-scatter.6.cloned.1.call-start = ((), (), s32[]{:S(2)}) async-start(), calls=%async_computation.2 | async-start | bytes 417792
  220.5 1.0 copy-start.4
  308.8 18.5 %collective-permute-start.6 = (f32[16,768]{1,0:T(8,128)S(1)}, f32[16,768]{1,0:T(8,128)S(1)}, u32[]{:S(2)}, u32[]{:S(2)}) collective-permute-start(f32[16,768]{1,0:T(8,128)S(1)} %fusion), channel_id=1, source_target_pairs={{0,7},{1,8},{2,9},{3,10},{4,11},{5,12},{6,13},{7,14},{8,15},{9,16}... | collective-permute-start | bytes 147464
  310.1 21.2 %collective-permute-start.5 = (f32[16,768]{1,0:T(8,128)S(1)}, f32[16,768]{1,0:T(8,128)S(1)}, u32[]{:S(2)}, u32[]{:S(2)}) collective-permute-start(f32[16,768]{1,0:T(8,128)S(1)} %fusion), channel_id=1, source_target_pairs={{0,6},{1,7},{2,8},{3,9},{4,10},{5,11},{6,12},{7,13},{8,14},{9,15},... | collective-permute-start | bytes 147464
  311.4 14.6 %collective-permute-start.7 = (f32[12,768]{1,0:T(8,128)S(1)}, f32[12,768]{1,0:T(8,128)S(1)}, u32[]{:S(2)}, u32[]{:S(2)}) collective-permute-start(f32[12,768]{1,0:T(8,128)S(1)} %slice.82), channel_id=1, source_target_pairs={{0,8},{1,9},{2,10},{3,11},{4,12},{5,13},{6,14},{7,15},{8,16},{9,17... | collective-permute-start | bytes 110600
  312.7 22.8 %collective-permute-start.4 = (f32[16,768]{1,0:T(8,128)S(1)}, f32[16,768]{1,0:T(8,128)S(1)}, u32[]{:S(2)}, u32[]{:S(2)}) collective-permute-start(f32[16,768]{1,0:T(8,128)S(1)} %fusion), channel_id=1, source_target_pairs={{0,5},{1,6},{2,7},{3,8},{4,9},{5,10},{6,11},{7,12},{8,13},{9,14},{... | collective-permute-start | bytes 147464
  314.0 21.5 %collective-permute-start.3 = (f32[16,768]{1,0:T(8,128)S(1)}, f32[16,768]{1,0:T(8,128)S(1)}, u32[]{:S(2)}, u32[]{:S(2)}) collective-permute-start(f32[16,768]{1,0:T(8,128)S(1)} %fusion), channel_id=1, source_target_pairs={{0,4},{1,5},{2,6},{3,7},{4,8},{5,9},{6,10},{7,11},{8,12},{9,13},{1... | collective-permute-start | bytes 147464
  326.0 9.5 %collective-permute-start.2 = (f32[16,768]{1,0:T(8,128)S(1)}, f32[16,768]{1,0:T(8,128)S(1)}, u32[]{:S(2)}, u32[]{:S(2)}) collective-permute-start(f32[16,768]{1,0:T(8,128)S(1)} %fusion), channel_id=1, source_target_pairs={{0,3},{1,4},{2,5},{3,6},{4,7},{5,8},{6,9},{7,10},{8,11},{9,12},{10... | collective-permute-start | bytes 147464
  327.3 8.2 %collective-permute-start.1 = (f32[16,768]{1,0:T(8,128)S(1)}, f32[16,768]{1,0:T(8,128)S(1)}, u32[]{:S(2)}, u32[]{:S(2)}) collective-permute-start(f32[16,768]{1,0:T(8,128)S(1)} %fusion), channel_id=1, source_target_pairs={{0,2},{1,3},{2,4},{3,5},{4,6},{5,7},{6,8},{7,9},{8,10},{9,11},{10,... | collective-permute-start | bytes 147464
  331.3 4.2 collective-permute-start
Sparse Core Ops, SparseCore 0:
  21.6 196.3 all-reduce.3
  337.7 109.1 reduce-scatter.5
where the time goes:
time: 457 us; the launch traced here: 455 us
  waiting for transfers between devices  305 us (67%)
  blocking collectives  86.3 us (19%)
  starting transfers between devices  24.7 us (5%)
  between operations  15.7 us (3%)
  other arithmetic  11.7 us (3%)
  local copies, waits for them, and re-layouts  6.59 us (1%)
  matrix products  5.5 us (1%)
    psum x1, waiting for transfers between devices, shards(): totals = lax.psum(partial_sum, 'seg')  196 us
    unnamed x11, waiting for transfers between devices  109 us
    unnamed x1, blocking collectives  86.3 us
    unnamed x9, starting transfers between devices  24.7 us
  transfers between devices with their start and end apart: 10, of which 2 were waited for; matrix products, arithmetic and copies ran while one was open for 0% of the time, Pallas kernels for 0%

commit v1 on v0

v1 whole, which is shorter than its diff:
```python
import functools
import math

import jax
import jax.numpy as jnp
import numpy as np
from jax import lax
from jax.experimental import pallas as pl
from jax.experimental.pallas import tpu as pltpu
from jax.sharding import PartitionSpec as P

SUBSTEPS = 4
NPIX = 384
SROWS = 256
SCOLS = 128
NSEG = 16
HALF = NSEG // 2
COILS = 32
OWN_ROWS = NPIX // COILS
OWN_COLS = 2 * NPIX // NSEG
MESH = pl.DeviceIdType.MESH
F32 = jnp.float32
BF16 = jnp.bfloat16
STRIP = 16


def dft_table():
    index = np.arange(NPIX)
    angle = (index[:, None] * index[None, :] % NPIX) * (2.0 * math.pi / NPIX)
    table = np.concatenate([np.cos(angle), np.sin(angle)], 0) / math.sqrt(NPIX)
    return table.astype(np.float32)


def dot_nt(lhs, rhs):
    return lax.dot_general(lhs, rhs, (((1,), (1,)), ((), ())), preferred_element_type=F32)


def dot_nn(lhs, rhs):
    return jnp.dot(lhs, rhs, preferred_element_type=F32)


def half_angle(field):
    y = field * 0.25
    z = y * y
    sine = y * (1.0 + z * (-1.0 / 6 + z * (1.0 / 120 + z * (-1.0 / 5040 + z * (1.0 / 362880)))))
    cosine = 1.0 + z * (-0.5 + z * (1.0 / 24 + z * (-1.0 / 720 + z * (1.0 / 40320 - z * (1.0 / 3628800)))))
    return 1.0 - 2.0 * sine * sine, 2.0 * sine * cosine


def hat(steps, segment):
    return jnp.maximum(0.0, 1.0 - jnp.abs(steps - float(segment * SUBSTEPS)) * (1.0 / SUBSTEPS))


def kernel(
    image_hbm,
    maps_hbm,
    field_hbm,
    rows_hbm,
    cols_hbm,
    measured_hbm,
    time_ref,
    count_ref,
    table_hbm,
    gradient_ref,
    residual_ref,
    image,
    maps,
    field,
    rows,
    cols,
    measured,
    table,
    base_re,
    base_im,
    cos_a,
    cos_b,
    sin_a,
    sin_b,
    twice,
    lhs_a,
    lhs_b,
    mix_b,
    mix_a,
    mix_at,
    stack_p,
    stack_q,
    weight_p,
    weight_m,
    samples,
    own_coil,
    own_cos_a,
    own_cos_b,
    own_sin_a,
    own_sin_b,
    own_twice,
    turned,
    image_sum,
    outbox,
    inbox,
    load_sem,
    send_sem,
    recv_sem,
):
    seg = lax.axis_index("seg")
    coil = lax.axis_index("coil")
    block = lax.rem(seg, HALF)
    component = lax.div(seg, HALF)

    barrier = pltpu.get_barrier_semaphore()

    def greet(step, carry):
        pl.semaphore_signal(
            barrier, inc=1, device_id={"coil": lax.rem(coil + step, COILS)}, device_id_type=MESH
        )
        return carry

    loads = [
        pltpu.make_async_copy(source, target, load_sem.at[place])
        for place, (source, target) in enumerate(
            [
                (table_hbm, table),
                (cols_hbm.at[0], cols),
                (field_hbm, field),
                (image_hbm.at[0], image),
                (maps_hbm.at[0], maps),
                (rows_hbm.at[0], rows),
                (measured_hbm.at[0, 0], measured),
            ]
        )
    ]
    for load in loads:
        load.start()
    lax.fori_loop(1, COILS, greet, 0)
    for load in loads:
        load.wait()

    col_mix = dot_nt(table[...], cols[...])
    cos_mix = col_mix[:NPIX].astype(BF16)
    sin_mix = col_mix[NPIX:].astype(BF16)
    mix_b[:NPIX, :SCOLS] = cos_mix
    mix_b[:NPIX, SCOLS:] = -sin_mix
    mix_b[NPIX : 2 * NPIX, :SCOLS] = sin_mix
    mix_b[NPIX : 2 * NPIX, SCOLS:] = cos_mix
    mix_b[2 * NPIX :, :] = jnp.zeros((16, 2 * SCOLS), BF16)
    mix_a[:, :NPIX] = dot_nn(rows[...], table[:NPIX]).astype(BF16)
    mix_a[:, NPIX:] = (-dot_nn(rows[...], table[NPIX:])).astype(BF16)
    row_mix = dot_nt(table[...], rows[...])
    mix_at[:, :SROWS] = row_mix[:NPIX].astype(BF16)
    mix_at[:, SROWS:] = (-row_mix[NPIX:]).astype(BF16)

    steps = jnp.transpose(jnp.broadcast_to(time_ref[...].astype(F32), (SCOLS, SROWS)))
    for pair in range(HALF):
        upper = hat(steps, HALF + pair)
        lower = hat(steps, HALF - 1 - pair)
        weight_p[pair] = upper + lower
        weight_m[pair] = upper - lower

    for start in range(0, NPIX, STRIP):
        at = slice(start, start + STRIP)
        im_re = image[at, :NPIX].astype(F32)
        im_im = image[at, NPIX:].astype(F32)
        co_re = maps[at, :NPIX].astype(F32)
        co_im = maps[at, NPIX:].astype(F32)
        base_re[at] = im_re * co_re - im_im * co_im
        base_im[at] = im_re * co_im + im_im * co_re
        cosine, sine = half_angle(field[at])
        cos_a[at] = cosine
        cos_b[at] = cosine
        sin_a[at] = sine
        sin_b[at] = -sine
        twice[at] = 4.0 * cosine * cosine - 2.0

    width = OWN_COLS
    pick_row = lax.broadcasted_iota(jnp.int32, (2 * NPIX, 128), 0)
    pick_lane = lax.broadcasted_iota(jnp.int32, (2 * NPIX, 128), 1)
    low = pick_lane < 64
    place = jnp.where(low, pick_lane, pick_lane - 64)
    wanted = place + width * block
    real_rows = wanted + jnp.where(low, component * NPIX, (1 - component) * NPIX)
    hit = (pick_row == real_rows) & (place < width)
    sign = jnp.where(low & (component == 1), -1.0, 1.0)
    pick_coil = jnp.where(hit, sign, 0.0).astype(BF16)
    own_coil[...] = dot_nn(maps[...], pick_coil)
    pick_field = jnp.where((pick_row == wanted) & (place < width), 1.0, 0.0)[:NPIX].astype(BF16)
    whole = field[...]
    high = whole.astype(BF16)
    rest = whole - high.astype(F32)
    middle = rest.astype(BF16)
    last = (rest - middle.astype(F32)).astype(BF16)
    own_field = dot_nn(high, pick_field) + dot_nn(middle, pick_field) + dot_nn(last, pick_field)
    cosine, sine = half_angle(own_field)
    own_cos_a[...] = cosine
    own_cos_b[...] = cosine
    own_sin_a[...] = sine
    own_sin_b[...] = -sine
    own_twice[...] = 4.0 * cosine * cosine - 2.0

    def phase_image(now_cos, other_cos, now_sin, other_sin, lhs):
        for start in range(0, NPIX, STRIP):
            at = slice(start, start + STRIP)
            below = slice(NPIX + start, NPIX + start + STRIP)
            cosine = now_cos[at]
            sine = now_sin[at]
            re = base_re[at]
            im = base_im[at]
            lhs[at, :NPIX] = (re * cosine).astype(BF16)
            lhs[at, NPIX:] = (im * cosine).astype(BF16)
            lhs[below, :NPIX] = (-im * sine).astype(BF16)
            lhs[below, NPIX:] = (re * sine).astype(BF16)
            double = twice[at]
            other_cos[at] = double * cosine - other_cos[at]
            other_sin[at] = double * sine - other_sin[at]

    def add_samples(lhs, pair):
        for part, (stack, weight) in enumerate([(stack_p, weight_p), (stack_q, weight_m)]):
            grid = dot_nn(lhs[part * NPIX : (part + 1) * NPIX], mix_b[: 2 * NPIX]).astype(BF16)
            stack[:NPIX] = grid
            stack[NPIX:, :SCOLS] = -grid[:, SCOLS:]
            stack[NPIX:, SCOLS:] = grid[:, :SCOLS]
        for stack, weight in [(stack_p, weight_p), (stack_q, weight_m)]:
            scale = weight[pair]
            found = dot_nn(mix_a[...], stack[...])
            samples[...] += jnp.concatenate([scale, scale], 1) * found

    samples[...] = jnp.zeros((SROWS, 2 * SCOLS), F32)
    phase_image(cos_a, cos_b, sin_a, sin_b, lhs_a)

    def forward(step, carry):
        phase_image(cos_b, cos_a, sin_b, sin_a, lhs_b)
        add_samples(lhs_a, 2 * step)
        phase_image(cos_a, cos_b, sin_a, sin_b, lhs_a)
        add_samples(lhs_b, 2 * step + 1)
        return carry

    lax.fori_loop(0, HALF // 2, forward, 0)

    row_ids = lax.broadcasted_iota(jnp.int32, (SROWS, 2 * SCOLS), 0)
    misfit = jnp.where(row_ids < count_ref[0], samples[...] - measured[...].astype(F32), 0.0)
    samples[...] = misfit
    share = SROWS // NSEG
    residual_ref[0, 0] = samples[pl.ds(pl.multiple_of(seg * share, share), share)]

    first = pl.multiple_of(block * width, 16)
    own_mix = jnp.concatenate([mix_b[pl.ds(first, 64)], mix_b[pl.ds(first + NPIX, 64)]], 0)
    turn = dot_nt(misfit.astype(BF16), own_mix)
    lane = lax.broadcasted_iota(jnp.int32, (SROWS, 128), 1)
    swapped = pltpu.roll(turn, 64, 1)
    turned[0] = turn
    turned[1] = jnp.where(lane < 64, swapped, -swapped)
    image_sum[...] = jnp.zeros((NPIX, 128), F32)

    def add_image(pair, now_cos, other_cos, now_sin, other_sin):
        plus = weight_p[pair]
        minus = weight_m[pair]
        top = jnp.concatenate([plus * turned[0], minus * turned[1]], 1)
        bottom = jnp.concatenate([plus * turned[1], -minus * turned[0]], 1)
        spread = jnp.concatenate([top, bottom], 0).astype(BF16)
        back = dot_nn(mix_at[...], spread)
        cosine = now_cos[...]
        sine = now_sin[...]
        image_sum[...] += cosine * back[:, :128] + sine * back[:, 128:]
        other_cos[...] = own_twice[...] * cosine - other_cos[...]
        other_sin[...] = own_twice[...] * sine - other_sin[...]

    def backward(step, carry):
        add_image(2 * step, own_cos_a, own_cos_b, own_sin_a, own_sin_b)
        add_image(2 * step + 1, own_cos_b, own_cos_a, own_sin_b, own_sin_a)
        return carry

    lax.fori_loop(0, HALF // 2, backward, 0)

    tile_lane = lax.broadcasted_iota(jnp.int32, (8, 128), 1)

    def folded(tile):
        at = slice(8 * tile, 8 * tile + 8)
        value = image_sum[at] * own_coil[at]
        return value + pltpu.roll(value, 64, 1)

    for pair in range(COILS // 2):
        shared = folded(3 * pair + 1)
        outbox[2 * pair] = jnp.where(tile_lane < 64, folded(3 * pair), shared)
        outbox[2 * pair + 1] = jnp.where(tile_lane < 64, folded(3 * pair + 2), shared)

    pl.semaphore_wait(barrier, COILS - 1)

    def send(step, carry):
        target = lax.rem(coil + step, COILS)
        pltpu.make_async_remote_copy(
            src_ref=outbox.at[target],
            dst_ref=inbox.at[step - 1],
            send_sem=send_sem,
            recv_sem=recv_sem,
            device_id={"coil": target},
            device_id_type=MESH,
        ).start()
        return carry

    lax.fori_loop(1, COILS, send, 0)
    everything = pltpu.make_async_remote_copy(
        src_ref=outbox.at[pl.ds(0, COILS - 1)],
        dst_ref=inbox,
        send_sem=send_sem,
        recv_sem=recv_sem,
        device_id={"coil": lax.rem(coil + 1, COILS)},
        device_id_type=MESH,
    )
    everything.wait_recv()
    total = outbox[coil]
    for slot in range(COILS - 1):
        total = total + inbox[slot]
    total = total * (COILS ** -0.5)
    high_lanes = pltpu.roll(total, 64, 1)
    even = jnp.concatenate([total, high_lanes[:4]], 0)
    odd = jnp.concatenate([high_lanes[4:], total], 0)
    result = jnp.where(lax.rem(coil, 2) == 0, even, odd)
    gradient_ref[0] = result[:, :OWN_COLS]
    everything.wait_send()


def shards(*arguments):
    vmem = pl.BlockSpec(memory_space=pltpu.VMEM)
    anywhere = pl.BlockSpec(memory_space=pl.ANY)
    smem = pl.BlockSpec(memory_space=pltpu.SMEM)
    square = pltpu.VMEM((NPIX, NPIX), F32)
    own = pltpu.VMEM((NPIX, 128), F32)
    return tuple(
        pl.pallas_call(
            kernel,
            out_shape=(
                jax.ShapeDtypeStruct((1, OWN_ROWS, OWN_COLS), F32),
                jax.ShapeDtypeStruct((1, 1, SROWS // NSEG, 2 * SCOLS), F32),
            ),
            in_specs=[anywhere] * 6 + [vmem, smem, anywhere],
            out_specs=(vmem, vmem),
            scratch_shapes=[
                pltpu.VMEM((NPIX, 2 * NPIX), BF16),
                pltpu.VMEM((NPIX, 2 * NPIX), BF16),
                square,
                pltpu.VMEM((SROWS, NPIX), BF16),
                pltpu.VMEM((SCOLS, NPIX), BF16),
                pltpu.VMEM((SROWS, 2 * SCOLS), BF16),
                pltpu.VMEM((2 * NPIX, NPIX), BF16),
                square,
                square,
                square,
                square,
                square,
                square,
                square,
                pltpu.VMEM((2 * NPIX, 2 * NPIX), BF16),
                pltpu.VMEM((2 * NPIX, 2 * NPIX), BF16),
                pltpu.VMEM((2 * NPIX + 16, 2 * SCOLS), BF16),
                pltpu.VMEM((SROWS, 2 * NPIX), BF16),
                pltpu.VMEM((NPIX, 2 * SROWS), BF16),
                pltpu.VMEM((2 * NPIX, 2 * SCOLS), BF16),
                pltpu.VMEM((2 * NPIX, 2 * SCOLS), BF16),
                pltpu.VMEM((HALF, SROWS, SCOLS), F32),
                pltpu.VMEM((HALF, SROWS, SCOLS), F32),
                pltpu.VMEM((SROWS, 2 * SCOLS), F32),
                own,
                own,
                own,
                own,
                own,
                own,
                pltpu.VMEM((2, SROWS, 128), F32),
                own,
                pltpu.VMEM((COILS, 8, 128), F32),
                pltpu.VMEM((COILS - 1, 8, 128), F32),
                pltpu.SemaphoreType.DMA((7,)),
                pltpu.SemaphoreType.DMA,
                pltpu.SemaphoreType.DMA,
            ],
            compiler_params=pltpu.CompilerParams(
                collective_id=0, has_side_effects=True, vmem_limit_bytes=48 * 2**20
            ),
        )(*arguments, jnp.asarray(dft_table()).astype(BF16))
    )


def solution(mesh):
    in_specs = (P(), P("coil", None, None), P(), P(), P(), P("coil", None, None, None), P(), P())
    out_specs = (P(None, "coil", "seg"), P("coil", None, "seg", None))
    return jax.shard_map(shards, mesh=mesh, in_specs=in_specs, out_specs=out_specs, check_vma=False)
```

time: 457 us -> 34.2 us (0.07)
  waiting for transfers between devices: 305 us -> 0 us
  blocking collectives: 86.3 us -> 0 us
  starting transfers between devices: 24.7 us -> 0 us
  Pallas kernels: 0 us -> 24.3 us
  between operations: 15.7 us -> 1.32 us
  other arithmetic: 11.7 us -> 0 us
  matrix products: 5.5 us -> 0 us
    psum x1 -> x0, waiting for transfers between devices: 196 us -> none  [shards(): totals = lax.psum(partial_sum, 'seg')]
    unnamed x11 -> x0, waiting for transfers between devices: 109 us -> none
    unnamed x1 -> x0, blocking collectives: 86.3 us -> none
    unnamed x9 -> x0, starting transfers between devices: 24.7 us -> none
    pallas_call x0 -> x1, Pallas kernels: none -> 24.3 us  [shards(): pl.pallas_call(kernel, out_shape=(jax.ShapeDtypeStruct((1, OWN_ROWS, OWN_...]
    another operation x6 -> x0, other arithmetic: 8.31 us -> none
    dot_general x7 -> x0, matrix products: 5.5 us -> none  [the longest x1 2.27 us: shards(): jnp.dot(interp_rows[0], kspace, preferred_element_type=jnp.float32)]
  transfers between devices with their start and end apart: 10 -> 0, of which waited for: 2 -> 0; matrix products, arithmetic and copies ran while one was open for 0% -> 0% of each run, Pallas kernels for 0% -> 0%
where the time goes in v1:
time: 34.2 us; the launch traced here: 33.8 us
  Pallas kernels  24.3 us (71%)
  local copies, waits for them, and re-layouts  8.19 us (24%)
  between operations  1.32 us (4%)
    pallas_call x1, Pallas kernels, shards(): pl.pallas_call(kernel, out_shape=(jax.ShapeDtypeStruct((1, OWN_ROWS, OWN_...  24.3 us
    unnamed x17, local copies, waits for them, and re-layouts  7.59 us

profile of v1, /device:TPU:1, one launch (start us, length us, event | category | flops | bytes accessed | tf_op | source)
XLA Modules:
  0.0 33.8 jit_solution(10449902056478528601)
XLA Ops:
  0.6 0.0 copy-start.7
  1.3 0.0 copy-done.7
  1.3 0.0 copy-start
  1.3 1.1 %copy-done = bf16[1,384,768]{2,1,0:T(8,128)(2,1)S(1)} copy-done((bf16[1,384,768]{2,1,0:T(8,128)(2,1)S(1)}, bf16[1,384,768]{2,1,0:T(8,128)(2,1)}, u32[]{:S(2)}) %copy-start) | copy-done | bytes 589848
  2.4 0.0 copy-start.1
  2.4 1.1 %copy-done.1 = bf16[1,384,768]{2,1,0:T(8,128)(2,1)S(1)} copy-done((bf16[1,384,768]{2,1,0:T(8,128)(2,1)S(1)}, bf16[1,384,768]{2,1,0:T(8,128)(2,1)}, u32[]{:S(2)}) %copy-start.1) | copy-done | bytes 589848
  3.4 0.0 copy-start.2
  3.4 1.1 %copy-done.2 = f32[384,384]{1,0:T(8,128)S(1)} copy-done((f32[384,384]{1,0:T(8,128)S(1)}, f32[384,384]{1,0:T(8,128)}, u32[]{:S(2)}) %copy-start.2) | copy-done | bytes 589848
  4.5 0.0 copy-start.3
  4.5 1.1 %copy-done.3 = bf16[768,384]{1,0:T(8,128)(2,1)S(1)} copy-done((bf16[768,384]{1,0:T(8,128)(2,1)S(1)}, bf16[768,384]{1,0:T(8,128)(2,1)}, u32[]{:S(2)}) %copy-start.3) | copy-done | bytes 589848
  5.6 0.0 copy-start.4
  5.6 0.9 %copy-done.4 = bf16[1,256,384]{2,1,0:T(8,128)(2,1)S(1)} copy-done((bf16[1,256,384]{2,1,0:T(8,128)(2,1)S(1)}, bf16[1,256,384]{2,1,0:T(8,128)(2,1)}, u32[]{:S(2)}) %copy-start.4) | copy-done | bytes 196632
  6.5 0.0 copy-start.5
  6.5 0.9 %copy-done.5 = bf16[1,1,256,256]{3,2,1,0:T(8,128)(2,1)S(1)} copy-done((bf16[1,1,256,256]{3,2,1,0:T(8,128)(2,1)S(1)}, bf16[1,1,256,256]{3,2,1,0:T(8,128)(2,1)}, u32[]{:S(2)}) %copy-start.5) | copy-done | bytes 131096
  7.4 0.0 copy-start.6
  7.4 0.9 %copy-done.6 = bf16[1,128,384]{2,1,0:T(8,128)(2,1)S(1)} copy-done((bf16[1,128,384]{2,1,0:T(8,128)(2,1)S(1)}, bf16[1,128,384]{2,1,0:T(8,128)(2,1)}, u32[]{:S(2)}) %copy-start.6) | copy-done | bytes 98328
  8.3 24.3 %shard_map.104 = (f32[1,12,48]{2,1,0:T(8,128)S(1)}, f32[1,1,16,256]{3,2,1,0:T(8,128)S(1)}) custom-call(bf16[1,384,768]{2,1,0:T(8,128)(2,1)S(1)} %copy-done, bf16[1,384,768]{2,1,0:T(8,128)(2,1)S(1)} %copy-done.1, f32[384,384]{1,0:T(8,128)S(1)} %copy-done.2, bf16[1,256,384]{2,1,0:T(8,128)(2,1)S(1)} %copy-done.4, bf16[1,128,384]{2,1,0:T(8,128)(2,1)S(1)} %copy-done.6, ...), custom_call_target="tpu_custom_call" | custom-call | tf_op jit(solution)/shard_map/pallas_call | solution.py:327
  32.6 0.6 %copy.11 = f32[1,12,48]{2,0,1:T(1,128)} copy(f32[1,12,48]{2,1,0:T(8,128)S(1)} %get-tuple-element.2) | data formatting | bytes 4608 | tf_op jit(solution)/shard_map/pallas_call | solution.py:327
  33.2 0.6 %copy.14 = f32[1,1,16,256]{3,2,1,0:T(8,128)} copy(f32[1,1,16,256]{3,2,1,0:T(8,128)S(1)} %get-tuple-element.7) | data formatting | bytes 32768
Async XLA Ops:
  0.6 0.7 %copy-start.7 = (s32[1,256]{1,0:T(1,128)S(1)}, s32[1,256]{1,0:T(1,128)}, u32[]{:S(2)}) copy-start(s32[1,256]{1,0:T(1,128)} %time_ref.1) | copy-start | bytes 3076
  1.3 1.1 %copy-start = (bf16[1,384,768]{2,1,0:T(8,128)(2,1)S(1)}, bf16[1,384,768]{2,1,0:T(8,128)(2,1)}, u32[]{:S(2)}) copy-start(bf16[1,384,768]{2,1,0:T(8,128)(2,1)} %image_hbm.1) | copy-start | bytes 1769476
  2.4 1.1 %copy-start.1 = (bf16[1,384,768]{2,1,0:T(8,128)(2,1)S(1)}, bf16[1,384,768]{2,1,0:T(8,128)(2,1)}, u32[]{:S(2)}) copy-start(bf16[1,384,768]{2,1,0:T(8,128)(2,1)} %maps_hbm.1) | copy-start | bytes 1769476
  3.4 1.1 %copy-start.2 = (f32[384,384]{1,0:T(8,128)S(1)}, f32[384,384]{1,0:T(8,128)}, u32[]{:S(2)}) copy-start(f32[384,384]{1,0:T(8,128)} %field_hbm.1) | copy-start | bytes 1769476
  4.5 1.1 %copy-start.3 = (bf16[768,384]{1,0:T(8,128)(2,1)S(1)}, bf16[768,384]{1,0:T(8,128)(2,1)}, u32[]{:S(2)}) copy-start(bf16[768,384]{1,0:T(8,128)(2,1)} %constant.5.table_hbm) | copy-start | bytes 1769476
  5.6 0.9 %copy-start.4 = (bf16[1,256,384]{2,1,0:T(8,128)(2,1)S(1)}, bf16[1,256,384]{2,1,0:T(8,128)(2,1)}, u32[]{:S(2)}) copy-start(bf16[1,256,384]{2,1,0:T(8,128)(2,1)} %rows_hbm.1) | copy-start | bytes 589828
  6.5 0.9 %copy-start.5 = (bf16[1,1,256,256]{3,2,1,0:T(8,128)(2,1)S(1)}, bf16[1,1,256,256]{3,2,1,0:T(8,128)(2,1)}, u32[]{:S(2)}) copy-start(bf16[1,1,256,256]{3,2,1,0:T(8,128)(2,1)} %measured_hbm.1) | copy-start | bytes 393220
  7.4 0.9 %copy-start.6 = (bf16[1,128,384]{2,1,0:T(8,128)(2,1)S(1)}, bf16[1,128,384]{2,1,0:T(8,128)(2,1)}, u32[]{:S(2)}) copy-start(bf16[1,128,384]{2,1,0:T(8,128)(2,1)} %cols_hbm.1) | copy-start | bytes 294916

commit v2 on v1

v2 whole, which is shorter than its diff:
```python
import functools
import math

import jax
import jax.numpy as jnp
import numpy as np
from jax import lax
from jax.experimental import pallas as pl
from jax.experimental.pallas import tpu as pltpu
from jax.sharding import PartitionSpec as P

SUBSTEPS = 4
NPIX = 384
SROWS = 256
SCOLS = 128
NSEG = 16
HALF = NSEG // 2
COILS = 32
OWN_ROWS = NPIX // COILS
OWN_COLS = 2 * NPIX // NSEG
MESH = pl.DeviceIdType.MESH
F32 = jnp.float32
BF16 = jnp.bfloat16
STRIP = 16
GROUP = 1


def dft_table():
    index = np.arange(NPIX)
    angle = (index[:, None] * index[None, :] % NPIX) * (2.0 * math.pi / NPIX)
    table = np.concatenate([np.cos(angle), np.sin(angle)], 0) / math.sqrt(NPIX)
    return table.astype(np.float32)


def dot_nt(lhs, rhs):
    return lax.dot_general(lhs, rhs, (((1,), (1,)), ((), ())), preferred_element_type=F32)


def dot_nn(lhs, rhs):
    return jnp.dot(lhs, rhs, preferred_element_type=F32)


def half_angle(field):
    y = field * 0.25
    z = y * y
    sine = y * (1.0 + z * (-1.0 / 6 + z * (1.0 / 120 + z * (-1.0 / 5040 + z * (1.0 / 362880)))))
    cosine = 1.0 + z * (-0.5 + z * (1.0 / 24 + z * (-1.0 / 720 + z * (1.0 / 40320 - z * (1.0 / 3628800)))))
    return 1.0 - 2.0 * sine * sine, 2.0 * sine * cosine


def hat(steps, segment):
    return jnp.maximum(0.0, 1.0 - jnp.abs(steps - float(segment * SUBSTEPS)) * (1.0 / SUBSTEPS))


def kernel(
    image_hbm,
    maps_hbm,
    field_hbm,
    rows_hbm,
    cols_hbm,
    measured_hbm,
    time_hbm,
    count_hbm,
    table_hbm,
    gradient_ref,
    residual_ref,
    image,
    maps,
    field,
    rows,
    cols,
    measured,
    table,
    time_ref,
    count_ref,
    base_re,
    base_im,
    cos_a,
    cos_b,
    sin_a,
    sin_b,
    twice,
    lhs_a,
    lhs_b,
    mix_b,
    mix_a,
    mix_at,
    grid_a,
    grid_b,
    quarters,
    weight_p,
    weight_m,
    samples,
    own_coil,
    own_cos_a,
    own_cos_b,
    own_sin_a,
    own_sin_b,
    own_twice,
    turned,
    image_sum,
    outbox,
    inbox,
    load_sem,
    send_sem,
    recv_sem,
):
    seg = lax.axis_index("seg")
    coil = lax.axis_index("coil")
    block = lax.rem(seg, HALF)
    component = lax.div(seg, HALF)

    barrier = pltpu.get_barrier_semaphore()

    def greet(step, carry):
        pl.semaphore_signal(
            barrier, inc=1, device_id={"coil": lax.rem(coil + step, COILS)}, device_id_type=MESH
        )
        return carry

    pairs = [
        (table_hbm, table),
        (cols_hbm.at[0], cols),
        (rows_hbm.at[0], rows),
        (time_hbm, time_ref),
        (field_hbm, field),
        (image_hbm.at[0], image),
        (maps_hbm.at[0], maps),
        (measured_hbm.at[0, 0], measured),
        (count_hbm, count_ref),
    ]
    loads = [
        pltpu.make_async_copy(source, target, load_sem.at[place])
        for place, (source, target) in enumerate(pairs)
    ]
    for load in loads:
        load.start()
    lax.fori_loop(1, COILS, greet, 0)
    for load in loads[:5]:
        load.wait()

    col_mix = dot_nt(table[...], cols[...])
    cos_mix = col_mix[:NPIX].astype(BF16)
    sin_mix = col_mix[NPIX:].astype(BF16)
    mix_b[:NPIX, :SCOLS] = cos_mix
    mix_b[:NPIX, SCOLS:] = -sin_mix
    mix_b[NPIX : 2 * NPIX, :SCOLS] = sin_mix
    mix_b[NPIX : 2 * NPIX, SCOLS:] = cos_mix
    mix_b[2 * NPIX :, :] = jnp.zeros((16, 2 * SCOLS), BF16)
    mix_a[:SROWS] = dot_nn(rows[...], table[:NPIX]).astype(BF16)
    mix_a[SROWS:] = (-dot_nn(rows[...], table[NPIX:])).astype(BF16)
    row_mix = dot_nt(table[...], rows[...])
    mix_at[:, :SROWS] = row_mix[:NPIX].astype(BF16)
    mix_at[:, SROWS:] = (-row_mix[NPIX:]).astype(BF16)

    steps = jnp.transpose(jnp.broadcast_to(time_ref[...].astype(F32), (SCOLS, SROWS)))
    for pair in range(HALF):
        upper = hat(steps, HALF + pair)
        lower = hat(steps, HALF - 1 - pair)
        weight_p[pair] = upper + lower
        weight_m[pair] = upper - lower

    for start in range(0, NPIX, STRIP):
        at = slice(start, start + STRIP)
        cosine, sine = half_angle(field[at])
        cos_a[at] = cosine
        cos_b[at] = cosine
        sin_a[at] = sine
        sin_b[at] = -sine
        twice[at] = 4.0 * cosine * cosine - 2.0

    width = OWN_COLS
    near = lax.div(block * width, 128)
    near_lane = pl.multiple_of(near * 128, 128)
    far_lane = pl.multiple_of(jnp.minimum(near + 1, NPIX // 128 - 1) * 128, 128)
    offset = block * width - near_lane
    back_turn = lax.rem(128 - offset, 128)
    whole_lane = lax.broadcasted_iota(jnp.int32, (NPIX, 128), 1)
    unbroken = whole_lane < 128 - offset

    def own_columns(near_half, far_half):
        return jnp.where(unbroken, pltpu.roll(near_half, back_turn, 1), pltpu.roll(far_half, back_turn, 1))

    def doubled(low, high):
        return jnp.where(whole_lane < 64, low, pltpu.roll(high, 64, 1))

    own_field = own_columns(field[:, pl.ds(near_lane, 128)], field[:, pl.ds(far_lane, 128)])
    own_field = doubled(own_field, own_field)
    cosine, sine = half_angle(own_field)
    own_cos_a[...] = cosine
    own_cos_b[...] = cosine
    own_sin_a[...] = sine
    own_sin_b[...] = -sine
    own_twice[...] = 4.0 * cosine * cosine - 2.0

    for load in loads[5:7]:
        load.wait()
    for start in range(0, NPIX, STRIP):
        at = slice(start, start + STRIP)
        im_re = image[at, :NPIX].astype(F32)
        im_im = image[at, NPIX:].astype(F32)
        co_re = maps[at, :NPIX].astype(F32)
        co_im = maps[at, NPIX:].astype(F32)
        base_re[at] = (im_re * co_re - im_im * co_im).astype(BF16)
        base_im[at] = (im_re * co_im + im_im * co_re).astype(BF16)

    def own_map(start):
        halves = [
            maps[:, pl.ds(pl.multiple_of(start + lane, 128), 128)].astype(F32)
            for lane in (near_lane, far_lane)
        ]
        return own_columns(*halves)

    map_re, map_im = own_map(0), own_map(NPIX)
    own_coil[...] = jnp.where(component == 0, doubled(map_re, map_im), doubled(-map_im, map_re))

    def phase_image(lhs):
        for start in range(0, NPIX, STRIP):
            at = slice(start, start + STRIP)
            re = base_re[at]
            im = base_im[at]
            double = twice[at]
            cosine, sine = cos_a[at], sin_a[at]
            last_cosine, last_sine = cos_b[at], sin_b[at]
            for pair in range(GROUP):
                plain = slice(2 * pair * NPIX + start, 2 * pair * NPIX + start + STRIP)
                below = slice(plain.start + NPIX, plain.stop + NPIX)
                short_cosine = cosine.astype(BF16)
                short_sine = sine.astype(BF16)
                lhs[plain, :NPIX] = re * short_cosine
                lhs[plain, NPIX:] = im * short_cosine
                lhs[below, :NPIX] = -im * short_sine
                lhs[below, NPIX:] = re * short_sine
                cosine, last_cosine = double * cosine - last_cosine, cosine
                sine, last_sine = double * sine - last_sine, sine
            cos_a[at], sin_a[at] = cosine, sine
            cos_b[at], sin_b[at] = last_cosine, last_sine

    def transform(lhs, grid):
        grid[...] = dot_nn(lhs[...], mix_b[: 2 * NPIX]).astype(BF16)

    def add_samples(grid, first):
        scales = []
        for pair in range(GROUP):
            for weight in (weight_p, weight_m):
                short = weight[first + pair].astype(BF16)
                scales.append(jnp.concatenate([jnp.concatenate([short] * 3, 1)] * 2, 0) * mix_a[...])
        quarters[...] += dot_nn(jnp.concatenate(scales, 1), grid[...])

    quarters[...] = jnp.zeros((2 * SROWS, 2 * SCOLS), F32)
    groups = HALF // GROUP
    both_lhs, both_grids = (lhs_a, lhs_b), (grid_a, grid_b)
    for step in range(groups + 2):
        if step < groups:
            phase_image(both_lhs[step % 2])
        if 0 < step <= groups:
            transform(both_lhs[(step - 1) % 2], both_grids[(step - 1) % 2])
        if step > 1:
            add_samples(both_grids[step % 2], (step - 2) * GROUP)
    top, bottom = quarters[:SROWS], quarters[SROWS:]
    samples[:, :SCOLS] = top[:, :SCOLS] - bottom[:, SCOLS:]
    samples[:, SCOLS:] = top[:, SCOLS:] + bottom[:, :SCOLS]

    for load in loads[7:]:
        load.wait()
    row_ids = lax.broadcasted_iota(jnp.int32, (SROWS, 2 * SCOLS), 0)
    misfit = jnp.where(row_ids < count_ref[0], samples[...] - measured[...].astype(F32), 0.0)
    samples[...] = misfit
    share = SROWS // NSEG
    residual_ref[0, 0] = samples[pl.ds(pl.multiple_of(seg * share, share), share)]

    first = pl.multiple_of(block * width, 16)
    own_mix = jnp.concatenate([mix_b[pl.ds(first, 64)], mix_b[pl.ds(first + NPIX, 64)]], 0)
    turn = dot_nt(misfit.astype(BF16), own_mix)
    lane = lax.broadcasted_iota(jnp.int32, (SROWS, 128), 1)
    swapped = pltpu.roll(turn, 64, 1)
    turned[0] = turn
    turned[1] = jnp.where(lane < 64, swapped, -swapped)
    image_sum[...] = jnp.zeros((NPIX, 128), F32)

    def add_image(pair, now_cos, other_cos, now_sin, other_sin):
        plus = weight_p[pair]
        minus = weight_m[pair]
        top = jnp.concatenate([plus * turned[0], minus * turned[1]], 1)
        bottom = jnp.concatenate([plus * turned[1], -minus * turned[0]], 1)
        spread = jnp.concatenate([top, bottom], 0).astype(BF16)
        back = dot_nn(mix_at[...], spread)
        cosine = now_cos[...]
        sine = now_sin[...]
        image_sum[...] += cosine * back[:, :128] + sine * back[:, 128:]
        other_cos[...] = own_twice[...] * cosine - other_cos[...]
        other_sin[...] = own_twice[...] * sine - other_sin[...]

    for pair in range(HALF):
        if pair % 2 == 0:
            add_image(pair, own_cos_a, own_cos_b, own_sin_a, own_sin_b)
        else:
            add_image(pair, own_cos_b, own_cos_a, own_sin_b, own_sin_a)

    value = image_sum[...] * own_coil[...]
    image_sum[...] = value + pltpu.roll(value, 64, 1)
    half = OWN_ROWS // 2
    tile_lane = lax.broadcasted_iota(jnp.int32, (half, 128), 1)
    for target in range(COILS):
        first_row = target * OWN_ROWS
        outbox[target] = jnp.where(
            tile_lane < 64,
            image_sum[first_row : first_row + half],
            image_sum[first_row + half : first_row + OWN_ROWS],
        )

    pl.semaphore_wait(barrier, COILS - 1)

    def send(step, carry):
        target = lax.rem(coil + step, COILS)
        pltpu.make_async_remote_copy(
            src_ref=outbox.at[target],
            dst_ref=inbox.at[step - 1],
            send_sem=send_sem,
            recv_sem=recv_sem,
            device_id={"coil": target},
            device_id_type=MESH,
        ).start()
        return carry

    lax.fori_loop(1, COILS, send, 0)
    everything = pltpu.make_async_remote_copy(
        src_ref=outbox.at[pl.ds(0, COILS - 1)],
        dst_ref=inbox,
        send_sem=send_sem,
        recv_sem=recv_sem,
        device_id={"coil": lax.rem(coil + 1, COILS)},
        device_id_type=MESH,
    )
    everything.wait_recv()
    total = outbox[coil]
    for slot in range(COILS - 1):
        total = total + inbox[slot]
    total = total * (COILS ** -0.5)
    gradient_ref[0, :half] = total[:, :OWN_COLS]
    gradient_ref[0, half:] = pltpu.roll(total, 64, 1)[:, :OWN_COLS]
    everything.wait_send()


def shards(*arguments):
    vmem = pl.BlockSpec(memory_space=pltpu.VMEM)
    anywhere = pl.BlockSpec(memory_space=pl.ANY)
    square = pltpu.VMEM((NPIX, NPIX), F32)
    own = pltpu.VMEM((NPIX, 128), F32)
    return tuple(
        pl.pallas_call(
            kernel,
            out_shape=(
                jax.ShapeDtypeStruct((1, OWN_ROWS, OWN_COLS), F32),
                jax.ShapeDtypeStruct((1, 1, SROWS // NSEG, 2 * SCOLS), F32),
            ),
            in_specs=[anywhere] * 9,
            out_specs=(vmem, vmem),
            scratch_shapes=[
                pltpu.VMEM((NPIX, 2 * NPIX), BF16),
                pltpu.VMEM((NPIX, 2 * NPIX), BF16),
                square,
                pltpu.VMEM((SROWS, NPIX), BF16),
                pltpu.VMEM((SCOLS, NPIX), BF16),
                pltpu.VMEM((SROWS, 2 * SCOLS), BF16),
                pltpu.VMEM((2 * NPIX, NPIX), BF16),
                pltpu.VMEM((1, SROWS), jnp.int32),
                pltpu.SMEM((1,), jnp.int32),
                pltpu.VMEM((NPIX, NPIX), BF16),
                pltpu.VMEM((NPIX, NPIX), BF16),
                square,
                square,
                square,
                square,
                square,
                pltpu.VMEM((2 * GROUP * NPIX, 2 * NPIX), BF16),
                pltpu.VMEM((2 * GROUP * NPIX, 2 * NPIX), BF16),
                pltpu.VMEM((2 * NPIX + 16, 2 * SCOLS), BF16),
                pltpu.VMEM((2 * SROWS, NPIX), BF16),
                pltpu.VMEM((NPIX, 2 * SROWS), BF16),
                pltpu.VMEM((2 * GROUP * NPIX, 2 * SCOLS), BF16),
                pltpu.VMEM((2 * GROUP * NPIX, 2 * SCOLS), BF16),
                pltpu.VMEM((2 * SROWS, 2 * SCOLS), F32),
                pltpu.VMEM((HALF, SROWS, SCOLS), F32),
                pltpu.VMEM((HALF, SROWS, SCOLS), F32),
                pltpu.VMEM((SROWS, 2 * SCOLS), F32),
                own,
                own,
                own,
                own,
                own,
                own,
                pltpu.VMEM((2, SROWS, 128), F32),
                own,
                pltpu.VMEM((COILS, OWN_ROWS // 2, 128), F32),
                pltpu.VMEM((COILS - 1, OWN_ROWS // 2, 128), F32),
                pltpu.SemaphoreType.DMA((9,)),
                pltpu.SemaphoreType.DMA,
                pltpu.SemaphoreType.DMA,
            ],
            compiler_params=pltpu.CompilerParams(
                collective_id=0, has_side_effects=True, vmem_limit_bytes=60 * 2**20
            ),
        )(*arguments, jnp.asarray(dft_table()).astype(BF16))
    )


def solution(mesh):
    in_specs = (P(), P("coil", None, None), P(), P(), P(), P("coil", None, None, None), P(), P())
    out_specs = (P(None, "coil", "seg"), P("coil", None, "seg", None))
    return jax.shard_map(shards, mesh=mesh, in_specs=in_specs, out_specs=out_specs, check_vma=False)
```

time: 34.2 us -> 25.7 us (0.75)
  local copies, waits for them, and re-layouts: 8.19 us -> 1.91 us
  Pallas kernels: 24.3 us -> 22.2 us
    unnamed x17 -> x3, local copies, waits for them, and re-layouts: 7.59 us -> 0.61 us
    pallas_call x1, Pallas kernels: 24.3 us -> 22.2 us  [shards(): pl.pallas_call(kernel, out_shape=(jax.ShapeDtypeStruct((1, OWN_ROWS, OWN_...]
    pallas_call x1, local copies, waits for them, and re-layouts: 0.6 us -> 1.3 us  [shards(): pl.pallas_call(kernel, out_shape=(jax.ShapeDtypeStruct((1, OWN_ROWS, OWN_...]
where the time goes in v2:
time: 25.7 us; the launch traced here: 25.5 us
  Pallas kernels  22.2 us (86%)
  local copies, waits for them, and re-layouts  1.91 us (7%)
  between operations  1.3 us (5%)
    pallas_call x1, Pallas kernels, shards(): pl.pallas_call(kernel, out_shape=(jax.ShapeDtypeStruct((1, OWN_ROWS, OWN_...  22.2 us
    pallas_call x1, local copies, waits for them, and re-layouts, shards(): pl.pallas_call(kernel, out_shape=(jax.ShapeDtypeStruct((1, OWN_ROWS, OWN_...  1.3 us
    unnamed x3, local copies, waits for them, and re-layouts  0.61 us

profile of v2, /device:TPU:1, one launch (start us, length us, event | category | flops | bytes accessed | tf_op | source)
XLA Modules:
  0.0 25.5 jit_solution(9332950336656438568)
XLA Ops:
  1.3 22.2 %shard_map.104 = (f32[1,12,48]{2,1,0:T(8,128)}, f32[1,1,16,256]{3,2,1,0:T(8,128)}) custom-call(bf16[1,384,768]{2,1,0:T(8,128)(2,1)} %image_hbm.1, bf16[1,384,768]{2,1,0:T(8,128)(2,1)} %maps_hbm.1, f32[384,384]{1,0:T(8,128)} %field_hbm.1, bf16[1,256,384]{2,1,0:T(8,128)(2,1)} %rows_hbm.1, bf16[1,128,384]{2,1,0:T(8,128)(2,1)} %cols_hbm.1, ...), custom_call_target="tpu_custom_call" | custom-call | tf_op jit(solution)/shard_map/pallas_call | solution.py:351
  23.5 0.0 copy-start
  23.5 1.3 %copy.11 = f32[1,12,48]{2,0,1:T(1,128)} copy(f32[1,12,48]{2,1,0:T(8,128)} %get-tuple-element.2) | data formatting | bytes 4608 | tf_op jit(solution)/shard_map/pallas_call | solution.py:351
  24.8 0.0 copy-done
  24.9 0.6 %copy.14 = f32[1,1,16,256]{3,2,1,0:T(8,128)} copy(f32[1,1,16,256]{3,2,1,0:T(8,128)S(1)} %copy-done) | data formatting | bytes 32768
Async XLA Ops:
  23.5 1.3 %copy-start = (f32[1,1,16,256]{3,2,1,0:T(8,128)S(1)}, f32[1,1,16,256]{3,2,1,0:T(8,128)}, u32[]{:S(2)}) copy-start(f32[1,1,16,256]{3,2,1,0:T(8,128)} %get-tuple-element.7) | copy-start | bytes 49156

commit v3 on v2

--- a/solution.py
+++ b/solution.py
@@ -22,7 +22,8 @@
 F32 = jnp.float32
 BF16 = jnp.bfloat16
 STRIP = 16
-GROUP = 1
+SPLIT = 1
+LOADS = 5 + 4 * SPLIT
 
 
 def dft_table():
@@ -98,6 +99,7 @@
     own_sin_b,
     own_twice,
     turned,
+    spread,
     image_sum,
     outbox,
     inbox,
@@ -118,27 +120,35 @@
         )
         return carry
 
-    pairs = [
-        (table_hbm, table),
-        (cols_hbm.at[0], cols),
-        (rows_hbm.at[0], rows),
-        (time_hbm, time_ref),
-        (field_hbm, field),
-        (image_hbm.at[0], image),
-        (maps_hbm.at[0], maps),
-        (measured_hbm.at[0, 0], measured),
-        (count_hbm, count_ref),
+    stages = [
+        [(table_hbm, table, 2 * NPIX), (cols_hbm.at[0], cols, 0), (rows_hbm.at[0], rows, 0)],
+        [(time_hbm, time_ref, 0), (field_hbm, field, NPIX)],
+        [(image_hbm.at[0], image, NPIX), (maps_hbm.at[0], maps, NPIX)],
+        [(measured_hbm.at[0, 0], measured, 0), (count_hbm, count_ref, 0)],
     ]
-    loads = [
-        pltpu.make_async_copy(source, target, load_sem.at[place])
-        for place, (source, target) in enumerate(pairs)
-    ]
-    for load in loads:
-        load.start()
+    loads = []
+    places = iter(range(LOADS))
+    for stage in stages:
+        loads.append([])
+        for source, target, length in stage:
+            pieces = [(source, target)]
+            if length:
+                piece = length // SPLIT
+                pieces = [
+                    (source.at[pl.ds(start, piece)], target.at[pl.ds(start, piece)])
+                    for start in range(0, length, piece)
+                ]
+            for piece_source, piece_target in pieces:
+                copy = pltpu.make_async_copy(piece_source, piece_target, load_sem.at[next(places)])
+                copy.start()
+                loads[-1].append(copy)
     lax.fori_loop(1, COILS, greet, 0)
-    for load in loads[:5]:
-        load.wait()
-
+
+    def arrived(stage):
+        for copy in loads[stage]:
+            copy.wait()
+
+    arrived(0)
     col_mix = dot_nt(table[...], cols[...])
     cos_mix = col_mix[:NPIX].astype(BF16)
     sin_mix = col_mix[NPIX:].astype(BF16)
@@ -153,6 +163,8 @@
     mix_at[:, :SROWS] = row_mix[:NPIX].astype(BF16)
     mix_at[:, SROWS:] = (-row_mix[NPIX:]).astype(BF16)
 
+    arrived(1)
+
     steps = jnp.transpose(jnp.broadcast_to(time_ref[...].astype(F32), (SCOLS, SROWS)))
     for pair in range(HALF):
         upper = hat(steps, HALF + pair)
@@ -193,8 +205,7 @@
     own_sin_b[...] = -sine
     own_twice[...] = 4.0 * cosine * cosine - 2.0
 
-    for load in loads[5:7]:
-        load.wait()
+    arrived(2)
     for start in range(0, NPIX, STRIP):
         at = slice(start, start + STRIP)
         im_re = image[at, :NPIX].astype(F32)
@@ -214,55 +225,50 @@
     map_re, map_im = own_map(0), own_map(NPIX)
     own_coil[...] = jnp.where(component == 0, doubled(map_re, map_im), doubled(-map_im, map_re))
 
-    def phase_image(lhs):
+    def phase_image(lhs, now_cos, other_cos, now_sin, other_sin):
         for start in range(0, NPIX, STRIP):
             at = slice(start, start + STRIP)
+            below = slice(NPIX + start, NPIX + start + STRIP)
             re = base_re[at]
             im = base_im[at]
+            cosine, sine = now_cos[at], now_sin[at]
+            short_cosine = cosine.astype(BF16)
+            short_sine = sine.astype(BF16)
+            lhs[at, :NPIX] = re * short_cosine
+            lhs[at, NPIX:] = im * short_cosine
+            lhs[below, :NPIX] = -im * short_sine
+            lhs[below, NPIX:] = re * short_sine
             double = twice[at]
-            cosine, sine = cos_a[at], sin_a[at]
-            last_cosine, last_sine = cos_b[at], sin_b[at]
-            for pair in range(GROUP):
-                plain = slice(2 * pair * NPIX + start, 2 * pair * NPIX + start + STRIP)
-                below = slice(plain.start + NPIX, plain.stop + NPIX)
-                short_cosine = cosine.astype(BF16)
-                short_sine = sine.astype(BF16)
-                lhs[plain, :NPIX] = re * short_cosine
-                lhs[plain, NPIX:] = im * short_cosine
-                lhs[below, :NPIX] = -im * short_sine
-                lhs[below, NPIX:] = re * short_sine
-                cosine, last_cosine = double * cosine - last_cosine, cosine
-                sine, last_sine = double * sine - last_sine, sine
-            cos_a[at], sin_a[at] = cosine, sine
-            cos_b[at], sin_b[at] = last_cosine, last_sine
+            other_cos[at] = double * cosine - other_cos[at]
+            other_sin[at] = double * sine - other_sin[at]
 
     def transform(lhs, grid):
         grid[...] = dot_nn(lhs[...], mix_b[: 2 * NPIX]).astype(BF16)
 
-    def add_samples(grid, first):
+    def add_samples(grid, pair):
         scales = []
-        for pair in range(GROUP):
-            for weight in (weight_p, weight_m):
-                short = weight[first + pair].astype(BF16)
-                scales.append(jnp.concatenate([jnp.concatenate([short] * 3, 1)] * 2, 0) * mix_a[...])
+        for weight in (weight_p, weight_m):
+            short = weight[pair].astype(BF16)
+            scales.append(jnp.concatenate([jnp.concatenate([short] * 3, 1)] * 2, 0) * mix_a[...])
         quarters[...] += dot_nn(jnp.concatenate(scales, 1), grid[...])
 
     quarters[...] = jnp.zeros((2 * SROWS, 2 * SCOLS), F32)
-    groups = HALF // GROUP
     both_lhs, both_grids = (lhs_a, lhs_b), (grid_a, grid_b)
-    for step in range(groups + 2):
-        if step < groups:
-            phase_image(both_lhs[step % 2])
-        if 0 < step <= groups:
+    for step in range(HALF + 2):
+        if step < HALF:
+            if step % 2 == 0:
+                phase_image(lhs_a, cos_a, cos_b, sin_a, sin_b)
+            else:
+                phase_image(lhs_b, cos_b, cos_a, sin_b, sin_a)
+        if 0 < step <= HALF:
             transform(both_lhs[(step - 1) % 2], both_grids[(step - 1) % 2])
         if step > 1:
-            add_samples(both_grids[step % 2], (step - 2) * GROUP)
+            add_samples(both_grids[step % 2], step - 2)
     top, bottom = quarters[:SROWS], quarters[SROWS:]
     samples[:, :SCOLS] = top[:, :SCOLS] - bottom[:, SCOLS:]
     samples[:, SCOLS:] = top[:, SCOLS:] + bottom[:, :SCOLS]
 
-    for load in loads[7:]:
-        load.wait()
+    arrived(3)
     row_ids = lax.broadcasted_iota(jnp.int32, (SROWS, 2 * SCOLS), 0)
     misfit = jnp.where(row_ids < count_ref[0], samples[...] - measured[...].astype(F32), 0.0)
     samples[...] = misfit
@@ -276,65 +282,70 @@
     swapped = pltpu.roll(turn, 64, 1)
     turned[0] = turn
     turned[1] = jnp.where(lane < 64, swapped, -swapped)
-    image_sum[...] = jnp.zeros((NPIX, 128), F32)
-
-    def add_image(pair, now_cos, other_cos, now_sin, other_sin):
+    for pair in range(HALF):
         plus = weight_p[pair]
         minus = weight_m[pair]
-        top = jnp.concatenate([plus * turned[0], minus * turned[1]], 1)
-        bottom = jnp.concatenate([plus * turned[1], -minus * turned[0]], 1)
-        spread = jnp.concatenate([top, bottom], 0).astype(BF16)
-        back = dot_nn(mix_at[...], spread)
-        cosine = now_cos[...]
-        sine = now_sin[...]
-        image_sum[...] += cosine * back[:, :128] + sine * back[:, 128:]
-        other_cos[...] = own_twice[...] * cosine - other_cos[...]
-        other_sin[...] = own_twice[...] * sine - other_sin[...]
-
-    for pair in range(HALF):
-        if pair % 2 == 0:
-            add_image(pair, own_cos_a, own_cos_b, own_sin_a, own_sin_b)
-        else:
-            add_image(pair, own_cos_b, own_cos_a, own_sin_b, own_sin_a)
-
-    value = image_sum[...] * own_coil[...]
-    image_sum[...] = value + pltpu.roll(value, 64, 1)
+        spread[pair, :SROWS, :128] = (plus * turned[0]).astype(BF16)
+        spread[pair, :SROWS, 128:] = (minus * turned[1]).astype(BF16)
+        spread[pair, SROWS:, :128] = (plus * turned[1]).astype(BF16)
+        spread[pair, SROWS:, 128:] = (-minus * turned[0]).astype(BF16)
+
+    rows_half = NPIX // 2
+    coils_half = COILS // 2
     half = OWN_ROWS // 2
-    tile_lane = lax.broadcasted_iota(jnp.int32, (half, 128), 1)
-    for target in range(COILS):
-        first_row = target * OWN_ROWS
-        outbox[target] = jnp.where(
-            tile_lane < 64,
-            image_sum[first_row : first_row + half],
-            image_sum[first_row + half : first_row + OWN_ROWS],
-        )
-
+    lanes = lax.broadcasted_iota(jnp.int32, (half, 128), 1)
+    own_half = lax.div(coil, coils_half)
+
+    def make_tiles(which):
+        at = pl.ds(pl.multiple_of(which * rows_half, rows_half), rows_half)
+        cosine, sine = own_cos_a[at], own_sin_a[at]
+        last_cosine, last_sine = own_cos_b[at], own_sin_b[at]
+        double = own_twice[at]
+        for pair in range(HALF):
+            back = dot_nn(mix_at[at], spread[pair])
+            term = cosine * back[:, :128] + sine * back[:, 128:]
+            image_sum[...] = term if pair == 0 else image_sum[...] + term
+            cosine, last_cosine = double * cosine - last_cosine, cosine
+            sine, last_sine = double * sine - last_sine, sine
+        value = image_sum[...] * own_coil[at]
+        image_sum[...] = value + pltpu.roll(value, 64, 1)
+        for place in range(coils_half):
+            first_row = place * OWN_ROWS
+            outbox[which * coils_half + place] = jnp.where(
+                lanes < 64,
+                image_sum[first_row : first_row + half],
+                image_sum[first_row + half : first_row + OWN_ROWS],
+            )
+
+    def send(which, first):
+        for step in range(first, coils_half):
+            target = which * coils_half + lax.rem(coil + step, coils_half)
+            pltpu.make_async_remote_copy(
+                src_ref=outbox.at[target],
+                dst_ref=inbox.at[coil],
+                send_sem=send_sem,
+                recv_sem=recv_sem,
+                device_id={"coil": target},
+                device_id_type=MESH,
+            ).start()
+
+    make_tiles(1 - own_half)
     pl.semaphore_wait(barrier, COILS - 1)
-
-    def send(step, carry):
-        target = lax.rem(coil + step, COILS)
-        pltpu.make_async_remote_copy(
-            src_ref=outbox.at[target],
-            dst_ref=inbox.at[step - 1],
-            send_sem=send_sem,
-            recv_sem=recv_sem,
-            device_id={"coil": target},
-            device_id_type=MESH,
-        ).start()
-        return carry
-
-    lax.fori_loop(1, COILS, send, 0)
+    send(1 - own_half, 0)
+    make_tiles(own_half)
+    send(own_half, 1)
+    inbox[coil] = outbox[coil]
     everything = pltpu.make_async_remote_copy(
         src_ref=outbox.at[pl.ds(0, COILS - 1)],
-        dst_ref=inbox,
+        dst_ref=inbox.at[pl.ds(0, COILS - 1)],
         send_sem=send_sem,
         recv_sem=recv_sem,
         device_id={"coil": lax.rem(coil + 1, COILS)},
         device_id_type=MESH,
     )
     everything.wait_recv()
-    total = outbox[coil]
-    for slot in range(COILS - 1):
+    total = inbox[0]
+    for slot in range(1, COILS):
         total = total + inbox[slot]
     total = total * (COILS ** -0.5)
     gradient_ref[0, :half] = total[:, :OWN_COLS]
@@ -373,13 +384,13 @@
                 square,
                 square,
                 square,
-                pltpu.VMEM((2 * GROUP * NPIX, 2 * NPIX), BF16),
-                pltpu.VMEM((2 * GROUP * NPIX, 2 * NPIX), BF16),
+                pltpu.VMEM((2 * NPIX, 2 * NPIX), BF16),
+                pltpu.VMEM((2 * NPIX, 2 * NPIX), BF16),
                 pltpu.VMEM((2 * NPIX + 16, 2 * SCOLS), BF16),
                 pltpu.VMEM((2 * SROWS, NPIX), BF16),
                 pltpu.VMEM((NPIX, 2 * SROWS), BF16),
-                pltpu.VMEM((2 * GROUP * NPIX, 2 * SCOLS), BF16),
-                pltpu.VMEM((2 * GROUP * NPIX, 2 * SCOLS), BF16),
+                pltpu.VMEM((2 * NPIX, 2 * SCOLS), BF16),
+                pltpu.VMEM((2 * NPIX, 2 * SCOLS), BF16),
                 pltpu.VMEM((2 * SROWS, 2 * SCOLS), F32),
                 pltpu.VMEM((HALF, SROWS, SCOLS), F32),
                 pltpu.VMEM((HALF, SROWS, SCOLS), F32),
@@ -391,10 +402,11 @@
                 own,
                 own,
                 pltpu.VMEM((2, SROWS, 128), F32),
-                own,
+                pltpu.VMEM((HALF, 2 * SROWS, 2 * 128), BF16),
+                pltpu.VMEM((NPIX // 2, 128), F32),
                 pltpu.VMEM((COILS, OWN_ROWS // 2, 128), F32),
-                pltpu.VMEM((COILS - 1, OWN_ROWS // 2, 128), F32),
-                pltpu.SemaphoreType.DMA((9,)),
+                pltpu.VMEM((COILS, OWN_ROWS // 2, 128), F32),
+                pltpu.SemaphoreType.DMA((LOADS,)),
                 pltpu.SemaphoreType.DMA,
                 pltpu.SemaphoreType.DMA,
             ],

time: 25.7 us -> 25.9 us (level)
  Pallas kernels: 22.2 us -> 22.5 us
where the time goes in v3:
time: 25.9 us; the launch traced here: 25.7 us
  Pallas kernels  22.5 us (87%)
  local copies, waits for them, and re-layouts  1.91 us (7%)
  between operations  1.3 us (5%)
    pallas_call x1, Pallas kernels, shards(): pl.pallas_call(kernel, out_shape=(jax.ShapeDtypeStruct((1, OWN_ROWS, OWN_...  22.5 us
    pallas_call x1, local copies, waits for them, and re-layouts, shards(): pl.pallas_call(kernel, out_shape=(jax.ShapeDtypeStruct((1, OWN_ROWS, OWN_...  1.3 us
    unnamed x3, local copies, waits for them, and re-layouts  0.61 us

profile of v3, /device:TPU:1, one launch (start us, length us, event | category | flops | bytes accessed | tf_op | source)
XLA Modules:
  0.0 25.7 jit_solution(15206531283178007142)
XLA Ops:
  1.3 22.5 %shard_map.104 = (f32[1,12,48]{2,1,0:T(8,128)}, f32[1,1,16,256]{3,2,1,0:T(8,128)}) custom-call(bf16[1,384,768]{2,1,0:T(8,128)(2,1)} %image_hbm.1, bf16[1,384,768]{2,1,0:T(8,128)(2,1)} %maps_hbm.1, f32[384,384]{1,0:T(8,128)} %field_hbm.1, bf16[1,256,384]{2,1,0:T(8,128)(2,1)} %rows_hbm.1, bf16[1,128,384]{2,1,0:T(8,128)(2,1)} %cols_hbm.1, ...), custom_call_target="tpu_custom_call" | custom-call | tf_op jit(solution)/shard_map/pallas_call | solution.py:362
  23.8 0.0 copy-start
  23.8 1.3 %copy.11 = f32[1,12,48]{2,0,1:T(1,128)} copy(f32[1,12,48]{2,1,0:T(8,128)} %get-tuple-element.2) | data formatting | bytes 4608 | tf_op jit(solution)/shard_map/pallas_call | solution.py:362
  25.1 0.0 copy-done
  25.1 0.6 %copy.14 = f32[1,1,16,256]{3,2,1,0:T(8,128)} copy(f32[1,1,16,256]{3,2,1,0:T(8,128)S(1)} %copy-done) | data formatting | bytes 32768
Async XLA Ops:
  23.8 1.3 %copy-start = (f32[1,1,16,256]{3,2,1,0:T(8,128)S(1)}, f32[1,1,16,256]{3,2,1,0:T(8,128)}, u32[]{:S(2)}) copy-start(f32[1,1,16,256]{3,2,1,0:T(8,128)} %get-tuple-element.7) | copy-start | bytes 49156

commit v4 on v2

v4 whole, which is shorter than its diff:
```python
import functools
import math

import jax
import jax.numpy as jnp
import numpy as np
from jax import lax
from jax.experimental import pallas as pl
from jax.experimental.pallas import tpu as pltpu
from jax.sharding import PartitionSpec as P

SUBSTEPS = 4
NPIX = 384
SROWS = 256
SCOLS = 128
NSEG = 16
HALF = NSEG // 2
COILS = 32
OWN_ROWS = NPIX // COILS
OWN_COLS = 2 * NPIX // NSEG
MESH = pl.DeviceIdType.MESH
F32 = jnp.float32
BF16 = jnp.bfloat16
STRIP = 16
BAND = 128
BANDS = NPIX // BAND
GROUPS = HALF // 2
T_PIECES = 2
I_PIECES = 2
LOADS = 6 + 3 * BANDS


def dft_table():
    index = np.arange(NPIX)
    angle = (index[:, None] * index[None, :] % NPIX) * (2.0 * math.pi / NPIX)
    table = np.concatenate([np.cos(angle), np.sin(angle)], 0) / math.sqrt(NPIX)
    return table.astype(np.float32)


def dot_nt(lhs, rhs):
    return lax.dot_general(lhs, rhs, (((1,), (1,)), ((), ())), preferred_element_type=F32)


def dot_nn(lhs, rhs):
    return jnp.dot(lhs, rhs, preferred_element_type=F32)


def half_angle(field):
    y = field * 0.25
    z = y * y
    sine = y * (1.0 + z * (-1.0 / 6 + z * (1.0 / 120 + z * (-1.0 / 5040 + z * (1.0 / 362880)))))
    cosine = 1.0 + z * (-0.5 + z * (1.0 / 24 + z * (-1.0 / 720 + z * (1.0 / 40320 - z * (1.0 / 3628800)))))
    return 1.0 - 2.0 * sine * sine, 2.0 * sine * cosine


def hat(steps, segment):
    return jnp.maximum(0.0, 1.0 - jnp.abs(steps - float(segment * SUBSTEPS)) * (1.0 / SUBSTEPS))


def kernel(
    image_hbm,
    maps_hbm,
    field_hbm,
    rows_hbm,
    cols_hbm,
    measured_hbm,
    time_hbm,
    count_hbm,
    table_hbm,
    gradient_ref,
    residual_ref,
    image,
    maps,
    field,
    rows,
    cols,
    measured,
    table,
    time_ref,
    count_ref,
    base_re,
    base_im,
    cosines,
    sines,
    mix_b,
    mix_a,
    mix_at,
    grid_a,
    grid_b,
    quarters,
    weight_p,
    weight_m,
    samples,
    own_coil,
    own_cos_a,
    own_cos_b,
    own_sin_a,
    own_sin_b,
    own_twice,
    turned,
    image_sum,
    outbox,
    inbox,
    load_sem,
    send_sem,
    recv_sem,
):
    seg = lax.axis_index("seg")
    coil = lax.axis_index("coil")
    block = lax.rem(seg, HALF)
    component = lax.div(seg, HALF)

    barrier = pltpu.get_barrier_semaphore()

    def greet(step, carry):
        pl.semaphore_signal(
            barrier, inc=1, device_id={"coil": lax.rem(coil + step, COILS)}, device_id_type=MESH
        )
        return carry

    def bands(source, target):
        return [(source.at[pl.ds(BAND * n, BAND)], target.at[pl.ds(BAND * n, BAND)]) for n in range(BANDS)]

    banded = list(
        zip(bands(field_hbm, field), bands(image_hbm.at[0], image), bands(maps_hbm.at[0], maps))
    )
    stages = [
        [(table_hbm, table), (cols_hbm.at[0], cols), *banded[0]],
        [(rows_hbm.at[0], rows), (time_hbm, time_ref)],
        *banded[1:],
        [(measured_hbm.at[0, 0], measured), (count_hbm, count_ref)],
    ]
    loads = []
    places = iter(range(LOADS))
    for stage in stages:
        loads.append([])
        for source, target in stage:
            copy = pltpu.make_async_copy(source, target, load_sem.at[next(places)])
            copy.start()
            loads[-1].append(copy)
    lax.fori_loop(1, COILS, greet, 0)

    def arrived(stage):
        for copy in loads[stage]:
            copy.wait()

    arrived(0)

    col_mix = dot_nt(table[...], cols[...])
    cos_mix = col_mix[:NPIX].astype(BF16)
    sin_mix = col_mix[NPIX:].astype(BF16)
    mix_b[:NPIX, :SCOLS] = cos_mix
    mix_b[:NPIX, SCOLS:] = -sin_mix
    mix_b[NPIX : 2 * NPIX, :SCOLS] = sin_mix
    mix_b[NPIX : 2 * NPIX, SCOLS:] = cos_mix
    mix_b[2 * NPIX :, :] = jnp.zeros((16, 2 * SCOLS), BF16)
    def prepare_rows():
        real = dot_nn(rows[...], table[:NPIX]).astype(BF16)
        negative = dot_nn(rows[...], table[NPIX:]).astype(BF16)
        mix_a[:SROWS] = real
        mix_a[SROWS : 2 * SROWS] = -negative
        mix_a[2 * SROWS : 3 * SROWS] = negative
        mix_a[3 * SROWS :] = real

        steps = jnp.transpose(jnp.broadcast_to(time_ref[...].astype(F32), (SCOLS, SROWS)))
        for pair in range(HALF):
            upper = hat(steps, HALF + pair)
            lower = hat(steps, HALF - 1 - pair)
            weight_p[pair] = upper + lower
            weight_m[pair] = upper - lower

    width = OWN_COLS

    near = lax.div(block * width, 128)
    near_lane = pl.multiple_of(near * 128, 128)
    far_lane = pl.multiple_of(jnp.minimum(near + 1, NPIX // 128 - 1) * 128, 128)
    offset = block * width - near_lane
    back_turn = lax.rem(128 - offset, 128)
    strip_lane = lax.broadcasted_iota(jnp.int32, (STRIP, 128), 1)
    unbroken = strip_lane < 128 - offset
    low_lanes = strip_lane < 64

    def prepare_own(start):
        at = slice(start, start + STRIP)

        def own_columns(ref, first):
            near_half = ref[at, pl.ds(pl.multiple_of(first + near_lane, 128), 128)].astype(F32)
            far_half = ref[at, pl.ds(pl.multiple_of(first + far_lane, 128), 128)].astype(F32)
            return jnp.where(
                unbroken, pltpu.roll(near_half, back_turn, 1), pltpu.roll(far_half, back_turn, 1)
            )

        def doubled(low, high):
            return jnp.where(low_lanes, low, pltpu.roll(high, 64, 1))

        own_field = own_columns(field, 0)
        cosine, sine = half_angle(doubled(own_field, own_field))
        own_cos_a[at] = cosine
        own_cos_b[at] = cosine
        own_sin_a[at] = sine
        own_sin_b[at] = -sine
        own_twice[at] = 4.0 * cosine * cosine - 2.0
        map_re, map_im = own_columns(maps, 0), own_columns(maps, NPIX)
        first = jnp.where(component == 0, map_re, -map_im)
        second = jnp.where(component == 0, map_im, map_re)
        own_coil[at] = doubled(first, second)

    def transpose_mix():
        row_mix = dot_nt(table[...], rows[...])
        mix_at[:, :SROWS] = row_mix[:NPIX].astype(BF16)
        mix_at[:, SROWS:] = (-row_mix[NPIX:]).astype(BF16)

    def prepare_strip(start):
        at = slice(start, start + STRIP)
        cosine, sine = half_angle(field[at])
        last_cosine, last_sine = cosine, -sine
        double = 4.0 * cosine * cosine - 2.0
        for pair in range(HALF):
            cosines[pair, at] = cosine.astype(BF16)
            sines[pair, at] = sine.astype(BF16)
            if pair < HALF - 1:
                cosine, last_cosine = double * cosine - last_cosine, cosine
                sine, last_sine = double * sine - last_sine, sine
        im_re = image[at, :NPIX].astype(F32)
        im_im = image[at, NPIX:].astype(F32)
        co_re = maps[at, :NPIX].astype(F32)
        co_im = maps[at, NPIX:].astype(F32)
        base_re[at] = (im_re * co_re - im_im * co_im).astype(BF16)
        base_im[at] = (im_re * co_im + im_im * co_re).astype(BF16)

    def transform(grid, band, group, piece, pieces):
        at = slice(BAND * band, BAND * (band + 1))
        re, im = base_re[at], base_im[at]
        parts = []
        each = 2 // pieces
        for pair in range(2 * group + each * piece, 2 * group + each * (piece + 1)):
            cosine, sine = cosines[pair, at], sines[pair, at]
            parts.append(jnp.concatenate([re * cosine, im * cosine], 1))
            parts.append(jnp.concatenate([re * sine, im * sine], 1))
        rows_each = 4 * BAND // pieces
        grid[piece * rows_each : (piece + 1) * rows_each] = dot_nn(
            jnp.concatenate(parts, 0), mix_b[: 2 * NPIX]
        ).astype(BF16)

    def add_samples(grid, band, group, piece, pieces):
        rows_each = 2 * SROWS // pieces
        at = slice(piece * rows_each, (piece + 1) * rows_each)
        start = piece * rows_each % SROWS
        band_at = slice(BAND * band, BAND * (band + 1))
        turned_at = slice(2 * SROWS + at.start, 2 * SROWS + at.stop)
        scales = []
        for pair in range(2):
            for weight, rows_at in ((weight_p, at), (weight_m, turned_at)):
                short = weight[2 * group + pair, start : start + rows_each].astype(BF16)
                scales.append(short * mix_a[rows_at, band_at])
        found = dot_nn(jnp.concatenate(scales, 1), grid[...])
        quarters[at] = found if band == group == 0 else quarters[at] + found

    for start in range(0, BAND, STRIP):
        prepare_strip(start)
    order = [(band, group) for band in range(BANDS) for group in range(GROUPS)]
    both_grids = (grid_a, grid_b)
    for step in range(len(order) + 1):
        jobs = []
        if step < len(order):
            band, group = order[step]
            if band + 1 < BANDS:
                if group == 0:
                    arrived(2 + band)
                each = BAND // GROUPS
                first = BAND * (band + 1) + each * group
                jobs = [functools.partial(prepare_strip, start) for start in range(first, first + each, STRIP)]
            else:
                each = NPIX // GROUPS
                first = each * group
                jobs = [functools.partial(prepare_own, start) for start in range(first, first + each, STRIP)]
        if step == 1:
            arrived(1)
            prepare_rows()
        work = []
        if step < len(order):
            work += [
                functools.partial(transform, both_grids[step % 2], *order[step], piece, T_PIECES)
                for piece in range(T_PIECES)
            ]
        if step > 0:
            work += [
                functools.partial(add_samples, both_grids[(step - 1) % 2], *order[step - 1], piece, I_PIECES)
                for piece in range(I_PIECES)
            ]
        if step == 2:
            work.append(transpose_mix)
        for slot, task in enumerate(work):
            for job in jobs[len(jobs) * slot // len(work) : len(jobs) * (slot + 1) // len(work)]:
                job()
            task()

    top, bottom = quarters[:SROWS], quarters[SROWS:]
    samples[:, :SCOLS] = top[:, :SCOLS] - bottom[:, SCOLS:]
    samples[:, SCOLS:] = top[:, SCOLS:] + bottom[:, :SCOLS]

    arrived(1 + BANDS)
    row_ids = lax.broadcasted_iota(jnp.int32, (SROWS, 2 * SCOLS), 0)
    misfit = jnp.where(row_ids < count_ref[0], samples[...] - measured[...].astype(F32), 0.0)
    samples[...] = misfit
    share = SROWS // NSEG
    residual_ref[...] = samples[pl.ds(pl.multiple_of(seg * share, share), share)]

    first = pl.multiple_of(block * width, 16)
    own_mix = jnp.concatenate([mix_b[pl.ds(first, 64)], mix_b[pl.ds(first + NPIX, 64)]], 0)
    turn = dot_nt(misfit.astype(BF16), own_mix)
    lane = lax.broadcasted_iota(jnp.int32, (SROWS, 128), 1)
    swapped = pltpu.roll(turn, 64, 1)
    turned[0] = turn
    turned[1] = jnp.where(lane < 64, swapped, -swapped)
    image_sum[...] = jnp.zeros((NPIX, 128), F32)

    def add_image(pair, now_cos, other_cos, now_sin, other_sin):
        plus = weight_p[pair]
        minus = weight_m[pair]
        top = jnp.concatenate([plus * turned[0], minus * turned[1]], 1)
        bottom = jnp.concatenate([plus * turned[1], -minus * turned[0]], 1)
        spread = jnp.concatenate([top, bottom], 0).astype(BF16)
        back = dot_nn(mix_at[...], spread)
        cosine = now_cos[...]
        sine = now_sin[...]
        image_sum[...] += cosine * back[:, :128] + sine * back[:, 128:]
        other_cos[...] = own_twice[...] * cosine - other_cos[...]
        other_sin[...] = own_twice[...] * sine - other_sin[...]

    for pair in range(HALF):
        if pair % 2 == 0:
            add_image(pair, own_cos_a, own_cos_b, own_sin_a, own_sin_b)
        else:
            add_image(pair, own_cos_b, own_cos_a, own_sin_b, own_sin_a)

    value = image_sum[...] * own_coil[...]
    image_sum[...] = value + pltpu.roll(value, 64, 1)
    half = OWN_ROWS // 2
    tile_lane = lax.broadcasted_iota(jnp.int32, (half, 128), 1)
    for target in range(COILS):
        first_row = target * OWN_ROWS
        outbox[target] = jnp.where(
            tile_lane < 64,
            image_sum[first_row : first_row + half],
            image_sum[first_row + half : first_row + OWN_ROWS],
        )

    pl.semaphore_wait(barrier, COILS - 1)

    def send(step, carry):
        target = lax.rem(coil + step, COILS)
        pltpu.make_async_remote_copy(
            src_ref=outbox.at[target],
            dst_ref=inbox.at[step - 1],
            send_sem=send_sem,
            recv_sem=recv_sem,
            device_id={"coil": target},
            device_id_type=MESH,
        ).start()
        return carry

    lax.fori_loop(1, COILS, send, 0)
    everything = pltpu.make_async_remote_copy(
        src_ref=outbox.at[pl.ds(0, COILS - 1)],
        dst_ref=inbox,
        send_sem=send_sem,
        recv_sem=recv_sem,
        device_id={"coil": lax.rem(coil + 1, COILS)},
        device_id_type=MESH,
    )
    everything.wait_recv()
    total = outbox[coil]
    for slot in range(COILS - 1):
        total = total + inbox[slot]
    total = total * (COILS ** -0.5)
    gradient_ref[:half] = total
    gradient_ref[half:] = total[:2]
    everything.wait_send()


def finish(total_ref, misfit_ref, gradient_ref, residual_ref):
    half = OWN_ROWS // 2
    total = total_ref[:half]
    gradient_ref[:half, 0] = total[:, :OWN_COLS]
    gradient_ref[half:, 0] = pltpu.roll(total, 64, 1)[:, :OWN_COLS]
    residual_ref[0, 0] = misfit_ref[...]


def shards(*arguments):
    vmem = pl.BlockSpec(memory_space=pltpu.VMEM)
    anywhere = pl.BlockSpec(memory_space=pl.ANY)
    square = pltpu.VMEM((NPIX, NPIX), F32)
    own = pltpu.VMEM((NPIX, 128), F32)
    total, misfit = (
        pl.pallas_call(
            kernel,
            out_shape=(
                jax.ShapeDtypeStruct((8, 128), F32),
                jax.ShapeDtypeStruct((SROWS // NSEG, 2 * SCOLS), F32),
            ),
            in_specs=[anywhere] * 9,
            out_specs=(vmem, vmem),
            scratch_shapes=[
                pltpu.VMEM((NPIX, 2 * NPIX), BF16),
                pltpu.VMEM((NPIX, 2 * NPIX), BF16),
                square,
                pltpu.VMEM((SROWS, NPIX), BF16),
                pltpu.VMEM((SCOLS, NPIX), BF16),
                pltpu.VMEM((SROWS, 2 * SCOLS), BF16),
                pltpu.VMEM((2 * NPIX, NPIX), BF16),
                pltpu.VMEM((1, SROWS), jnp.int32),
                pltpu.SMEM((1,), jnp.int32),
                pltpu.VMEM((NPIX, NPIX), BF16),
                pltpu.VMEM((NPIX, NPIX), BF16),
                pltpu.VMEM((HALF, NPIX, NPIX), BF16),
                pltpu.VMEM((HALF, NPIX, NPIX), BF16),
                pltpu.VMEM((2 * NPIX + 16, 2 * SCOLS), BF16),
                pltpu.VMEM((4 * SROWS, NPIX), BF16),
                pltpu.VMEM((NPIX, 2 * SROWS), BF16),
                pltpu.VMEM((4 * BAND, 2 * SCOLS), BF16),
                pltpu.VMEM((4 * BAND, 2 * SCOLS), BF16),
                pltpu.VMEM((2 * SROWS, 2 * SCOLS), F32),
                pltpu.VMEM((HALF, SROWS, SCOLS), F32),
                pltpu.VMEM((HALF, SROWS, SCOLS), F32),
                pltpu.VMEM((SROWS, 2 * SCOLS), F32),
                own,
                own,
                own,
                own,
                own,
                own,
                pltpu.VMEM((2, SROWS, 128), F32),
                own,
                pltpu.VMEM((COILS, OWN_ROWS // 2, 128), F32),
                pltpu.VMEM((COILS - 1, OWN_ROWS // 2, 128), F32),
                pltpu.SemaphoreType.DMA((LOADS,)),
                pltpu.SemaphoreType.DMA,
                pltpu.SemaphoreType.DMA,
            ],
            compiler_params=pltpu.CompilerParams(
                collective_id=0, has_side_effects=True, vmem_limit_bytes=60 * 2**20
            ),
        )(*arguments, jnp.asarray(dft_table()).astype(BF16))
    )

    gradient, residual = pl.pallas_call(
        finish,
        out_shape=(
            jax.ShapeDtypeStruct((OWN_ROWS, 1, OWN_COLS), F32),
            jax.ShapeDtypeStruct((1, 1, SROWS // NSEG, 2 * SCOLS), F32),
        ),
        in_specs=[vmem, vmem],
        out_specs=(vmem, vmem),
    )(total, misfit)
    return jnp.transpose(gradient, (1, 0, 2)), residual


def solution(mesh):
    in_specs = (P(), P("coil", None, None), P(), P(), P(), P("coil", None, None, None), P(), P())
    out_specs = (P(None, "coil", "seg"), P("coil", None, "seg", None))
    return jax.shard_map(shards, mesh=mesh, in_specs=in_specs, out_specs=out_specs, check_vma=False)
```

time: 25.7 us -> 23.9 us (0.930)
  local copies, waits for them, and re-layouts: 1.91 us -> 0 us
    pallas_call x1 -> x0, local copies, waits for them, and re-layouts: 1.3 us -> none  [shards(): pl.pallas_call(kernel, out_shape=(jax.ShapeDtypeStruct((1, OWN_ROWS, OWN_...]
    unnamed x3 -> x0, local copies, waits for them, and re-layouts: 0.61 us -> none
    pallas_call x1 -> x2, Pallas kernels: 22.2 us -> 22.4 us  [the longest x1 21 us: shards(): pl.pallas_call(kernel, out_shape=(jax.ShapeDtypeStruct((8, 128), F32), ja...]
where the time goes in v4:
time: 23.9 us; the launch traced here: 23.7 us
  Pallas kernels  22.4 us (94%)
  between operations  1.29 us (5%)
    pallas_call x1, Pallas kernels, shards(): pl.pallas_call(kernel, out_shape=(jax.ShapeDtypeStruct((8, 128), F32), ja...  21 us
    pallas_call x1, Pallas kernels, shards(): pl.pallas_call(finish, out_shape=(jax.ShapeDtypeStruct((OWN_ROWS, 1, OWN_...  1.39 us

profile of v4, /device:TPU:1, one launch (start us, length us, event | category | flops | bytes accessed | tf_op | source)
XLA Modules:
  0.0 23.7 jit_solution(12283014123579263054)
XLA Ops:
  1.3 21.0 %shard_map.104 = (f32[8,128]{1,0:T(8,128)}, f32[16,256]{1,0:T(8,128)}) custom-call(bf16[1,384,768]{2,1,0:T(8,128)(2,1)} %image_hbm.1, bf16[1,384,768]{2,1,0:T(8,128)(2,1)} %maps_hbm.1, f32[384,384]{1,0:T(8,128)} %field_hbm.1, bf16[1,256,384]{2,1,0:T(8,128)(2,1)} %rows_hbm.1, bf16[1,128,384]{2,1,0:T(8,128)(2,1)} %cols_hbm.1, ...), custom_call_target="tpu_custom_call" | custom-call | tf_op jit(solution)/shard_map/pallas_call | solution.py:396
  22.3 1.4 %shard_map.105 = (f32[12,1,48]{2,1,0:T(1,128)}, f32[1,1,16,256]{3,2,1,0:T(8,128)}) custom-call(f32[8,128]{1,0:T(8,128)} %get-tuple-element.6.total_ref, f32[16,256]{1,0:T(8,128)} %get-tuple-element.7.misfit_ref), custom_call_target="tpu_custom_call" | custom-call | tf_op jit(solution)/shard_map/pallas_call | solution.py:447

commit v5 on v4

--- a/solution.py
+++ b/solution.py
@@ -439,7 +439,7 @@
                 pltpu.SemaphoreType.DMA,
             ],
             compiler_params=pltpu.CompilerParams(
-                collective_id=0, has_side_effects=True, vmem_limit_bytes=60 * 2**20
+                collective_id=0, has_side_effects=True, vmem_limit_bytes=55160 * 2**10
             ),
         )(*arguments, jnp.asarray(dft_table()).astype(BF16))
     )
@@ -452,6 +452,7 @@
         ),
         in_specs=[vmem, vmem],
         out_specs=(vmem, vmem),
+        compiler_params=pltpu.CompilerParams(vmem_limit_bytes=1 * 2**20),
     )(total, misfit)
     return jnp.transpose(gradient, (1, 0, 2)), residual
 

time: 23.9 us -> 22.5 us (0.941)
  Pallas kernels: 22.4 us -> 21 us
    pallas_call x1, Pallas kernels: 1.39 us -> 0.67 us  [shards(): pl.pallas_call(finish, out_shape=(jax.ShapeDtypeStruct((OWN_ROWS, 1, OWN_...]
    pallas_call x1, Pallas kernels: 21 us -> 20.4 us  [shards(): pl.pallas_call(kernel, out_shape=(jax.ShapeDtypeStruct((8, 128), F32), ja...]
where the time goes in v5:
time: 22.5 us; the launch traced here: 22.4 us
  Pallas kernels  21 us (93%)
  between operations  1.31 us (6%)
    pallas_call x1, Pallas kernels, shards(): pl.pallas_call(kernel, out_shape=(jax.ShapeDtypeStruct((8, 128), F32), ja...  20.4 us
    pallas_call x1, Pallas kernels, shards(): pl.pallas_call(finish, out_shape=(jax.ShapeDtypeStruct((OWN_ROWS, 1, OWN_...  0.67 us

profile of v5, /device:TPU:1, one launch (start us, length us, event | category | flops | bytes accessed | tf_op | source)
XLA Modules:
  0.0 22.4 jit_solution(18066967353583165339)
XLA Ops:
  0.6 0.0 copy-start
  1.3 0.0 copy-done
  1.3 20.4 %shard_map.104 = (f32[8,128]{1,0:T(8,128)S(1)}, f32[16,256]{1,0:T(8,128)S(1)}) custom-call(bf16[1,384,768]{2,1,0:T(8,128)(2,1)} %image_hbm.1, bf16[1,384,768]{2,1,0:T(8,128)(2,1)} %maps_hbm.1, f32[384,384]{1,0:T(8,128)} %field_hbm.1, bf16[1,256,384]{2,1,0:T(8,128)(2,1)} %rows_hbm.1, bf16[1,128,384]{2,1,0:T(8,128)(2,1)} %cols_hbm.1, ...), custom_call_target="tpu_custom_call" | custom-call | tf_op jit(solution)/shard_map/pallas_call | solution.py:396
  21.7 0.7 %shard_map.105 = (f32[12,1,48]{2,1,0:T(1,128)}, f32[1,1,16,256]{3,2,1,0:T(8,128)}) custom-call(f32[8,128]{1,0:T(8,128)S(1)} %get-tuple-element.6.total_ref, f32[16,256]{1,0:T(8,128)S(1)} %get-tuple-element.7.misfit_ref), custom_call_target="tpu_custom_call" | custom-call | tf_op jit(solution)/shard_map/pallas_call | solution.py:447
Async XLA Ops:
  0.6 0.7 %copy-start = (s32[1,256]{1,0:T(1,128)S(1)}, s32[1,256]{1,0:T(1,128)}, u32[]{:S(2)}) copy-start(s32[1,256]{1,0:T(1,128)} %time_hbm.1) | copy-start | bytes 3076

commit v6 on v5

--- a/solution.py
+++ b/solution.py
@@ -360,7 +360,8 @@
         ).start()
         return carry
 
-    lax.fori_loop(1, COILS, send, 0)
+    for step in range(1, COILS):
+        send(step, 0)
     everything = pltpu.make_async_remote_copy(
         src_ref=outbox.at[pl.ds(0, COILS - 1)],
         dst_ref=inbox,

time: 22.5 us -> 22.5 us (level)
  no operation moved by 1% of the time
where the time goes in v6:
time: 22.5 us; the launch traced here: 22.4 us
  Pallas kernels  21 us (93%)
  between operations  1.31 us (6%)
    pallas_call x1, Pallas kernels, shards(): pl.pallas_call(kernel, out_shape=(jax.ShapeDtypeStruct((8, 128), F32), ja...  20.4 us
    pallas_call x1, Pallas kernels, shards(): pl.pallas_call(finish, out_shape=(jax.ShapeDtypeStruct((OWN_ROWS, 1, OWN_...  0.67 us

profile of v6, /device:TPU:1, one launch (start us, length us, event | category | flops | bytes accessed | tf_op | source)
XLA Modules:
  0.0 22.4 jit_solution(4248126002382235591)
XLA Ops:
  0.6 0.0 copy-start
  1.3 0.0 copy-done
  1.3 20.4 %shard_map.104 = (f32[8,128]{1,0:T(8,128)S(1)}, f32[16,256]{1,0:T(8,128)S(1)}) custom-call(bf16[1,384,768]{2,1,0:T(8,128)(2,1)} %image_hbm.1, bf16[1,384,768]{2,1,0:T(8,128)(2,1)} %maps_hbm.1, f32[384,384]{1,0:T(8,128)} %field_hbm.1, bf16[1,256,384]{2,1,0:T(8,128)(2,1)} %rows_hbm.1, bf16[1,128,384]{2,1,0:T(8,128)(2,1)} %cols_hbm.1, ...), custom_call_target="tpu_custom_call" | custom-call | tf_op jit(solution)/shard_map/pallas_call | solution.py:397
  21.7 0.7 %shard_map.105 = (f32[12,1,48]{2,1,0:T(1,128)}, f32[1,1,16,256]{3,2,1,0:T(8,128)}) custom-call(f32[8,128]{1,0:T(8,128)S(1)} %get-tuple-element.6.total_ref, f32[16,256]{1,0:T(8,128)S(1)} %get-tuple-element.7.misfit_ref), custom_call_target="tpu_custom_call" | custom-call | tf_op jit(solution)/shard_map/pallas_call | solution.py:448
Async XLA Ops:
  0.6 0.7 %copy-start = (s32[1,256]{1,0:T(1,128)S(1)}, s32[1,256]{1,0:T(1,128)}, u32[]{:S(2)}) copy-start(s32[1,256]{1,0:T(1,128)} %time_hbm.1) | copy-start | bytes 3076
